TPU v7x, 256 devices: a whole 4x4x8 slice. The times are simulated.
256 devices in a mesh: wide: 16 (over x_hi, z), narrow: 16 (over x_lo, y, core).
Axes of the slice: x: 4 (x_hi: 2, x_lo: 2; x = x_hi * 2 + x_lo), y: 4, z: 8, core: 2. Of those that a mesh axis runs over, the one named last changes fastest.
Arguments:
- pair_act: bfloat16 [768, 768, 128], P('wide', 'narrow'), may hold values from -6 to 6
- residue_mask: int32 [768], replicated, may hold values 0 or 1
- w_proj_start: bfloat16 [128, 512], replicated, may hold values from -0.5 to 0.5
- w_bias_start: bfloat16 [128, 4], replicated, may hold values from -40 to 40
- w_out_start: bfloat16 [128, 128], replicated, may hold values from -0.5 to 0.5
- w_proj_end: bfloat16 [128, 512], replicated, may hold values from -0.5 to 0.5
- w_bias_end: bfloat16 [128, 4], replicated, may hold values from -40 to 40
- w_out_end: bfloat16 [128, 128], replicated, may hold values from -0.5 to 0.5
Outputs:
- update_start: bfloat16 [768, 768, 128], P('wide', 'narrow')
- update_end: bfloat16 [768, 768, 128], P('wide', 'narrow')
All inputs are finite; a program needn't handle non-finite values.
Results may differ from a plain program's by a relative error of at most 0.012.
The roundings to bfloat16 on the way count: a program that leaves them out, or rounds other values in their place, can miss the bound.
Values may be sent and summed in bfloat16 or wider, within the bound.
A program may use at most 64 MiB of HBM per device.

v0:
```python
import jax
import jax.numpy as jnp
from jax import lax
from jax.sharding import Mesh
from jax.sharding import PartitionSpec as P

NARROW = ("narrow_0", "narrow_1", "narrow_2")


norm_eps = 1e-05
masked_score = -1000000000.0


def cut_along(x, dim, count):
    before, after = (x.shape[:dim], x.shape[dim + 1 :])
    return jnp.moveaxis(x.reshape(*before, count, -1, *after), dim, 0)


def in_order(parts, dim):
    parts = jnp.moveaxis(parts, 0, dim)
    shape = parts.shape
    return parts.reshape(*shape[:dim], shape[dim] * shape[dim + 1], *shape[dim + 2 :])


def turned_blocks(parts, axes, order):
    inside = parts.shape[1:]
    out = parts.reshape(*(lax.axis_size(a) for a in axes), *inside)
    for k in order:
        out = lax.all_to_all(out, axes[k], k, k, tiled=True)
    return out.reshape(-1, *inside)


def two_step_exchange(x, groups, order, split_dim, concat_dim):
    count = lax.axis_size(groups[0]) * lax.axis_size(groups[1])
    parts = cut_along(x, split_dim, count)
    return in_order(turned_blocks(parts, groups, order), concat_dim)


def layer_norm(features):
    average = jnp.mean(features, axis=-1, keepdims=True)
    centred = features - average
    spread = jnp.mean(centred * centred, axis=-1, keepdims=True)
    return (centred * lax.rsqrt(spread + norm_eps)).astype(jnp.bfloat16)


def attend(projected, pair_bias, row_ok, key_ok, head_count, head_dim):
    length = projected.shape[1]
    inv_root = head_dim ** (-0.5)

    def one_row(item_pair):
        packed, valid_row = item_pair
        packed = packed.reshape(length, head_count, 4, head_dim)
        queries = packed[:, :, 0]
        keyset = packed[:, :, 1]
        values = packed[:, :, 2]
        gating = packed[:, :, 3]
        scores = (
            jnp.einsum("bhd,khd->hbk", queries, keyset, preferred_element_type=jnp.float32)
            * inv_root
            + pair_bias
        )
        allowed = jnp.logical_and(valid_row, key_ok)
        scores = jnp.where(allowed[None, None, :], scores, masked_score)
        weights = jax.nn.softmax(scores, axis=-1).astype(jnp.bfloat16)
        summed = jnp.einsum("hbk,khd->bhd", weights, values, preferred_element_type=jnp.float32)
        gated = (jax.nn.sigmoid(gating.astype(jnp.float32)) * summed).astype(jnp.bfloat16)
        return gated.reshape(length, head_count * head_dim)

    return lax.map(one_row, (projected, row_ok))


def on_device(
    pair_act,
    residue_mask,
    w_proj_start,
    w_bias_start,
    w_out_start,
    w_proj_end,
    w_bias_end,
    w_out_end,
):
    wide_count = lax.axis_size("wide")
    narrow_count = lax.axis_size(NARROW)
    wide_at = lax.axis_index("wide")
    narrow_at = lax.axis_index(NARROW)
    tile_rows, tile_cols, channels = pair_act.shape
    head_count = w_bias_start.shape[1]
    head_dim = w_out_start.shape[0] // head_count
    residue_ok = residue_mask > 0
    normed = layer_norm(pair_act.astype(jnp.float32))
    groups = narrow_count // head_count
    sub_rows = tile_rows // groups
    proj_tile = jnp.einsum(
        "ijc,chx->hijx",
        normed,
        w_proj_start.reshape(channels, head_count, -1),
        preferred_element_type=jnp.float32,
    ).astype(jnp.bfloat16)
    outgoing = proj_tile.reshape(narrow_count, sub_rows, tile_cols, -1)
    bias_tile = jnp.einsum("ijc,ch->hij", normed, w_bias_start, preferred_element_type=jnp.float32)
    bias_out = jnp.repeat(bias_tile, groups, axis=0)
    incoming = two_step_exchange(outgoing, (("narrow_0", "narrow_1"), "narrow_2"), (1, 0), 0, 2)
    bias_rows = lax.all_to_all(bias_out, NARROW, split_axis=0, concat_axis=2, tiled=True)
    pair_bias = lax.all_gather(bias_rows, "wide", axis=1, tiled=True)
    group_at = narrow_at % groups
    first_row = wide_at * tile_rows + group_at * sub_rows
    row_ok = lax.dynamic_slice_in_dim(residue_ok, first_row, sub_rows)
    gated = attend(incoming[0], pair_bias, row_ok, residue_ok, 1, head_dim)
    returned = lax.all_to_all(
        gated.reshape(sub_rows, -1), NARROW, split_axis=1, concat_axis=0, tiled=True
    )
    head_tile = returned.reshape(head_count, tile_rows, tile_cols, head_dim)
    update_start = jnp.einsum(
        "hijd,hdc->ijc",
        head_tile,
        w_out_start.reshape(head_count, head_dim, channels),
        preferred_element_type=jnp.float32,
    ).astype(jnp.bfloat16)
    updated = pair_act.astype(jnp.float32) + update_start.astype(jnp.float32)
    normed_end = layer_norm(updated)
    groups_wide = wide_count // head_count
    sub_cols = tile_cols // groups_wide
    proj_end_tile = jnp.einsum(
        "ijc,chx->hjix",
        normed_end,
        w_proj_end.reshape(channels, head_count, -1),
        preferred_element_type=jnp.float32,
    ).astype(jnp.bfloat16)
    outgoing_end = proj_end_tile.reshape(wide_count, sub_cols, tile_rows, -1)
    bias_end_tile = jnp.einsum(
        "ijc,ch->hji", normed_end, w_bias_end, preferred_element_type=jnp.float32
    )
    bias_end_out = jnp.repeat(bias_end_tile, groups_wide, axis=0)
    incoming_end = lax.all_to_all(outgoing_end, "wide", split_axis=0, concat_axis=2, tiled=True)
    bias_cols = lax.all_to_all(bias_end_out, "wide", split_axis=0, concat_axis=2, tiled=True)
    pair_bias_end = lax.all_gather(bias_cols, NARROW, axis=1, tiled=True)
    group_wide = wide_at % groups_wide
    first_col = narrow_at * tile_cols + group_wide * sub_cols
    col_ok = lax.dynamic_slice_in_dim(residue_ok, first_col, sub_cols)
    gated_end = attend(incoming_end[0], pair_bias_end, col_ok, residue_ok, 1, head_dim)
    returned_end = lax.all_to_all(
        gated_end.reshape(sub_cols, -1), "wide", split_axis=1, concat_axis=0, tiled=True
    )
    head_tile_end = returned_end.reshape(head_count, tile_cols, tile_rows, head_dim)
    update_end = jnp.einsum(
        "hjid,hdc->ijc",
        head_tile_end,
        w_out_end.reshape(head_count, head_dim, channels),
        preferred_element_type=jnp.float32,
    ).astype(jnp.bfloat16)
    return (update_start, update_end)


def solution(mesh):
    split = Mesh(
        mesh.devices.reshape(mesh.shape["wide"], 2, 4, 2),
        ("wide", "narrow_0", "narrow_1", "narrow_2"),
    )
    placed = (P("wide", NARROW, None), P(), P(), P(), P(), P(), P(), P())
    return jax.shard_map(
        on_device,
        mesh=split,
        in_specs=placed,
        out_specs=(P("wide", NARROW, None), P("wide", NARROW, None)),
        check_vma=False,
    )
```

profile of v0, /device:TPU:1, one launch (start us, length us, event | category | flops | bytes accessed | tf_op | source)
XLA Modules:
  0.0 377.7 jit_solution(18101503657099255865)
XLA Ops:
  7.2 1.5 convert_reduce_fusion
  8.7 1.8 fusion.21
  10.5 1.9 convolution_bitcast_fusion.3
  12.9 13.0 %all_to_all.95 = f32[16,1,2304]{2,1,0:T(1,128)S(1)} all-to-all(f32[16,1,2304]{2,1,0:T(1,128)S(1)} %reshape.255), channel_id=1, replica_groups=mesh['wide'=16,'narrow_0'=2,'narrow_1'=4,'narrow_2'=2] {'narrow_0','narr..., dimensions={0} | all-to-all | bytes 294912 | tf_op jit(solution)/shard_map/all_to_all | solution.py:103
  27.8 1.0 all_to_all.86
  28.9 1.1 convert_bitcast_fusion.1
  30.8 6.0 %all_to_all.96 = bf16[8,2,1,12,48,128]{5,4,3,0,2,1:T(8,128)(2,1)S(1)} all-to-all(bf16[8,2,1,12,48,128]{5,4,3,0,2,1:T(8,128)(2,1)S(1)} %copy.76), channel_id=1, replica_groups=mesh['wide'=16,'narrow_0'=2,'narrow_1'=4,'narrow_2'=2] {'narrow_2'}, dimensions={1} | all-to-all | bytes 4718592 | tf_op jit(solution)/shard_map/all_to_all | solution.py:29
  36.8 1.8 copy.77
  38.6 3.8 all-to-all-start.1
  42.5 29.1 %all-to-all-done.1 = bf16[8,2,1,12,48,128]{5,4,3,1,2,0:T(8,128)(2,1)S(1)} async-done(((bf16[8,2,1,12,48,128]{5,4,3,1,2,0:T(8,128)(2,1)}), bf16[8,2,1,12,48,128]{5,4,3,1,2,0:T(8,128)(2,1)S(1)}, u32[]{:S(2)}, u32[]{:S(2)}) %all-to-all-start.1) | async-done | bytes 2359328 | tf_op jit(solution)/shard_map/all_to_all | solution.py:29
  71.6 2.0 copy.78
  73.6 39.9 %all-gather.3.cloned.1.call-done = f32[1,768,768]{2,0,1:T(1,128)} async-done(((f32[1,48,768]{2,0,1:T(1,128)}), f32[1,768,768]{2,0,1:T(1,128)}) %all-gather.3.cloned.1.call-update) | async-done | bytes 2359312 | tf_op jit(solution)/shard_map/all_gather | solution.py:104
  113.5 5.5 %copy.83 = f32[1,768,768]{1,2,0:T(8,128)S(1)} copy(f32[1,768,768]{2,0,1:T(1,128)} %all-gather.3.cloned.1.call-done) | data formatting | bytes 4718592 | tf_op jit(solution)/shard_map/while | solution.py:69
  119.8 52.3 %while.20 = (s32[]{:T(128)}, bf16[12,768,32]{1,2,0:T(8,128)(2,1)}, bf16[12,768,128]{2,1,0:T(8,128)(2,1)}, pred[12]{0:T(512)(128)(4,1)S(1)}, pred[768]{0:T(1024)(...) while((s32[]{:T(128)}, bf16[12,768,32]{1,2,0:T(8,128)(2,1)}, bf16[12,768,128]{2,1,0:T(8,128)(2,1)}, ...), condition=%wide.region_5.6_spmd, body=%wide.region_2.5_spmd.sunk | while | flops 80952576 | bytes 10489944 | solution.py:69
  123.0 1.1 fusion.50
  127.4 1.1 fusion.50
  131.7 1.1 fusion.50
  136.1 1.1 fusion.50
  140.5 1.1 fusion.50
  144.8 1.1 fusion.50
  149.2 1.1 fusion.50
  153.5 1.1 fusion.50
  157.9 1.1 fusion.50
  162.2 1.1 fusion.50
  166.6 1.1 fusion.50
  171.0 1.1 fusion.50
  172.1 2.0 copy.84
  174.2 3.0 all_to_all.73
  177.2 1.4 copy.85
  178.6 21.3 %all_to_all.97 = bf16[12,16,1536]{2,0,1:T(8,128)(2,1)} all-to-all(bf16[12,16,1536]{2,0,1:T(8,128)(2,1)S(1)} %copy.85), channel_id=1, replica_groups=mesh['wide'=16,'narrow_0'=2,'narrow_1'=4,'narrow_2'=2] {'narrow_0','narr..., dimensions={1} | all-to-all | bytes 1179648 | tf_op jit(solution)/shard_map/all_to_all | solution.py:109
  199.9 3.0 reshape.234
  202.9 1.4 fusion.24
  206.3 1.0 reshape.257
  207.4 5.7 %all-to-all-start.5 = ((f32[16,1,2304]{2,1,0:T(1,128)}), f32[16,1,2304]{2,1,0:T(1,128)S(1)}, u32[]{:S(2)}, u32[]{:S(2)}) async-start(f32[16,1,2304]{2,1,0:T(1,128)} %reshape.257), calls=%async_computation.5 | async-start | bytes 294912 | tf_op jit(solution)/shard_map/all_to_all | solution.py:135
  213.1 1.9 convert_bitcast_fusion
  215.0 2.9 copy.88
  217.9 4.2 %all-to-all-done.5 = f32[16,1,2304]{2,1,0:T(1,128)S(1)} async-done(((f32[16,1,2304]{2,1,0:T(1,128)}), f32[16,1,2304]{2,1,0:T(1,128)S(1)}, u32[]{:S(2)}, u32[]{:S(2)}) %all-to-all-start.5) | async-done | bytes 147488 | tf_op jit(solution)/shard_map/all_to_all | solution.py:135
  222.1 4.9 %all-to-all-start.4 = ((bf16[16,12,48,128]{3,2,1,0:T(8,128)(2,1)}), bf16[16,12,48,128]{3,2,1,0:T(8,128)(2,1)S(1)}, u32[]{:S(2)}, u32[]{:S(2)}) async-start(bf16[16,12,48,128]{3,2,1,0:T(8,128)(2,1)} %bitcast.42), calls=%async_computation.4 | async-start | bytes 4718592 | tf_op jit(solution)/shard_map/all_to_all | solution.py:134
  228.6 1.0 all_to_all.87
  229.6 52.7 %all-to-all-done.4 = bf16[16,12,48,128]{3,2,1,0:T(8,128)(2,1)S(1)} async-done(((bf16[16,12,48,128]{3,2,1,0:T(8,128)(2,1)}), bf16[16,12,48,128]{3,2,1,0:T(8,128)(2,1)S(1)}, u32[]{:S(2)}, u32[]{:S(2)}) %all-to-all-start.4) | async-done | bytes 2359328 | tf_op jit(solution)/shard_map/all_to_all | solution.py:134
  282.3 2.0 copy.89
  284.3 5.5 %copy.94 = f32[1,768,768]{1,2,0:T(8,128)S(1)} copy(f32[1,768,768]{2,0,1:T(1,128)} %all-gather.5.cloned.1.call-done) | data formatting | bytes 4718592 | tf_op jit(solution)/shard_map/while | solution.py:69
  289.8 46.0 %while.21 = (s32[]{:T(128)}, bf16[12,768,32]{1,2,0:T(8,128)(2,1)S(1)}, bf16[12,768,128]{2,1,0:T(8,128)(2,1)}, pred[12]{0:T(512)(128)(4,1)S(1)}, pred[768]{0:T(10...) while((s32[]{:T(128)}, bf16[12,768,32]{1,2,0:T(8,128)(2,1)S(1)}, ...), condition=%wide.region_11.12_spmd, body=%wide.region_8.11_spmd.sunk | while | flops 80952576 | bytes 10489436 | solution.py:69
  335.8 1.1 copy.95
  337.0 2.3 all_to_all.83
  339.7 27.5 %all_to_all.98 = bf16[12,16,1536]{2,0,1:T(8,128)(2,1)S(1)} all-to-all(bf16[12,16,1536]{2,0,1:T(8,128)(2,1)S(1)} %copy.96), channel_id=1, replica_groups=mesh['wide'=16,'narrow_0'=2,'narrow_1'=4,'narrow_2'=2] {'wide'}, dimensions={1} | all-to-all | bytes 1179648 | tf_op jit(solution)/shard_map/all_to_all | solution.py:141
  367.1 1.6 reshape.239
  368.7 1.1 fusion.20
  (203 shorter events, 93.2 us)
Async XLA Ops:
  7.2 21.7 %copy-start = (bf16[128,512]{1,0:T(8,128)(2,1)S(1)}, bf16[128,512]{1,0:T(8,128)(2,1)}, u32[]{:S(2)}) copy-start(bf16[128,512]{1,0:T(8,128)(2,1)} %param.14) | copy-start | bytes 393220
  7.2 106.3 %all-gather.3.cloned.1.call-start = ((), (), s32[]{:S(2)}) async-start(), calls=%async_computation.7 | async-start | bytes 2506752 | tf_op jit(solution)/shard_map/all_gather | solution.py:104
  10.5 18.4 %copy-start.1 = (bf16[48,48,128]{2,1,0:T(8,128)(2,1)S(1)}, bf16[48,48,128]{2,1,0:T(8,128)(2,1)}, u32[]{:S(2)}) copy-start(bf16[48,48,128]{2,1,0:T(8,128)(2,1)} %param.12) | copy-start | bytes 1769476
  38.6 3.8 %copy-start.6 = (s32[768]{0:T(1024)S(1)}, s32[768]{0:T(1024)}, u32[]{:S(2)}) copy-start(s32[768]{0:T(1024)} %param.13) | copy-start | bytes 9220
  38.6 33.0 %all-to-all-start.1 = ((bf16[8,2,1,12,48,128]{5,4,3,1,2,0:T(8,128)(2,1)}), bf16[8,2,1,12,48,128]{5,4,3,1,2,0:T(8,128)(2,1)S(1)}, u32[]{:S(2)}, u32[]{:S(2)}) async-start(bf16[8,2,1,12,48,128]{5,4,3,1,2,0:T(8,128)(2,1)} %copy.77), calls=%async_computation.1 | async-start | bytes 4718592 | tf_op jit(solution)/shard_map/all_to_all | solution.py:29
  178.6 24.3 %copy-start.4 = (bf16[128,128]{1,0:T(8,128)(2,1)S(1)}, bf16[128,128]{1,0:T(8,128)(2,1)}, u32[]{:S(2)}) copy-start(bf16[128,128]{1,0:T(8,128)(2,1)} %param.16) | copy-start | bytes 98308
  202.9 2.3 copy-start.7
  204.3 0.8 copy-start.2
  204.3 8.7 %copy-start.3 = (bf16[128,512]{1,0:T(8,128)(2,1)S(1)}, bf16[128,512]{1,0:T(8,128)(2,1)}, u32[]{:S(2)}) copy-start(bf16[128,512]{1,0:T(8,128)(2,1)} %param.17) | copy-start | bytes 393220
  207.4 14.7 %all-to-all-start.5 = ((f32[16,1,2304]{2,1,0:T(1,128)}), f32[16,1,2304]{2,1,0:T(1,128)S(1)}, u32[]{:S(2)}, u32[]{:S(2)}) async-start(f32[16,1,2304]{2,1,0:T(1,128)} %reshape.257), calls=%async_computation.5 | async-start | bytes 294912 | tf_op jit(solution)/shard_map/all_to_all | solution.py:135
  222.1 60.2 %all-to-all-start.4 = ((bf16[16,12,48,128]{3,2,1,0:T(8,128)(2,1)}), bf16[16,12,48,128]{3,2,1,0:T(8,128)(2,1)S(1)}, u32[]{:S(2)}, u32[]{:S(2)}) async-start(bf16[16,12,48,128]{3,2,1,0:T(8,128)(2,1)} %bitcast.42), calls=%async_computation.4 | async-start | bytes 4718592 | tf_op jit(solution)/shard_map/all_to_all | solution.py:134
  227.0 57.3 %all-gather.5.cloned.1.call-start = ((), (), s32[]{:S(2)}) async-start(), calls=%async_computation.8 | async-start | bytes 2506752 | tf_op jit(solution)/shard_map/all_gather | solution.py:136
  339.7 29.1 %copy-start.5 = (bf16[128,128]{1,0:T(8,128)(2,1)S(1)}, bf16[128,128]{1,0:T(8,128)(2,1)}, u32[]{:S(2)}) copy-start(bf16[128,128]{1,0:T(8,128)(2,1)} %param.19) | copy-start | bytes 98308
Sparse Core Ops, SparseCore 0:
  29.0 84.4 all-gather.2
  230.2 42.5 all-gather.4
where the time goes:
time: 382 us; the launch traced here: 378 us
  waiting for transfers between devices  126 us (33%)
  local copies, waits for them, and re-layouts  82.4 us (22%)
  blocking collectives  67.7 us (18%)
  matrix products  42.6 us (11%)
  other arithmetic  29.4 us (8%)
  starting transfers between devices  14.6 us (4%)
  between operations  14.5 us (4%)
    all_to_all x1, waiting for transfers between devices, on_device(): lax.all_to_all(outgoing_end, 'wide', split_axis=0, concat_axis=2, tiled=T...  52.7 us
    dynamic_slice x72, local copies, waits for them, and re-layouts, attend(): return lax.map(one_row, (projected, row_ok))  40.2 us
    all_gather x1, waiting for transfers between devices, on_device(): pair_bias = lax.all_gather(bias_rows, 'wide', axis=1, tiled=True)  39.9 us
    all_to_all x1, waiting for transfers between devices, turned_blocks(): out = lax.all_to_all(out, axes[k], k, k, tiled=True)  29.1 us
    all_to_all x1, blocking collectives, on_device(): lax.all_to_all(gated_end.reshape(sub_cols, -1), 'wide', split_axis=1, con...  27.5 us
    all_to_all x1, blocking collectives, on_device(): lax.all_to_all(gated.reshape(sub_rows, -1), NARROW, split_axis=1, concat_...  21.3 us
    dot_general x24, matrix products, one_row(): jnp.einsum('hbk,khd->bhd', weights, values, preferred_element_type=jnp.fl...  19.8 us
    and x24, other arithmetic, one_row(): allowed = jnp.logical_and(valid_row, key_ok)  14.6 us
  transfers between devices with their start and end apart: 5, of which 4 were waited for; matrix products, arithmetic and copies ran while one was open for 4% of the time, Pallas kernels for 0%

commit v1 on v0

v1 whole, which is shorter than its diff:
```python
import functools
import math

import jax
import jax.numpy as jnp
import numpy as np
from jax import lax
from jax.experimental import pallas as pl
from jax.experimental.pallas import tpu as pltpu
from jax.sharding import Mesh
from jax.sharding import PartitionSpec as P

AXES = ("xh", "z", "xl", "y", "c")
SIZES = (2, 8, 2, 4, 2)
NARROW = ("xl", "y", "c")
WIDE = ("xh", "z")

HEADS = 4
DIM = 32
CH = HEADS * DIM
TILE = 48
N = 768
ROWS = 6
SUPER = 4
POS = 2 * TILE
EXP = POS * HEADS
SUB = 192
NORM_EPS = 1e-05
MASKED = -1000000000.0
INV_ROOT = DIM ** (-0.5)
ROOT = math.sqrt(DIM)
LOG2E = math.log2(math.e)
BF = jnp.bfloat16
F32 = jnp.float32


def layer_norm(features):
    average = jnp.mean(features, axis=-1, keepdims=True)
    centred = features - average
    spread = jnp.mean(centred * centred, axis=-1, keepdims=True)
    return (centred * lax.rsqrt(spread + NORM_EPS)).astype(BF)


def here():
    return {a: lax.axis_index(a) for a in AXES}


def place(at, **kw):
    return tuple(kw.get(a, at[a]) for a in AXES)


def dot(a, b, dims):
    return lax.dot_general(a, b, (dims, ((), ())), preferred_element_type=F32)


NN = ((1,), (0,))
NT = ((1,), (1,))


def send(src, dst, ssem, rsem, device):
    return pltpu.make_async_remote_copy(
        src_ref=src,
        dst_ref=dst,
        send_sem=ssem,
        recv_sem=rsem,
        device_id=device,
        device_id_type=pl.DeviceIdType.MESH,
    )


class Ring:
    def __init__(self, n, idx, whole, halves, plus, minus, ssem, rsem, base):
        self.n, self.idx = n, idx
        self.whole, self.halves = whole, halves
        self.plus, self.minus = plus, minus
        self.ssem, self.rsem, self.base = ssem, rsem, base
        self.sent = []

    def block(self, offset):
        return lax.rem(self.idx + offset + self.n, self.n)

    def copy(self, step, way, region):
        at = self.base + 2 * (step - 1) + way
        return send(region, region, self.ssem.at[at], self.rsem.at[at], self.minus if way else self.plus)

    def go(self, step, way, region):
        copy = self.copy(step, way, region)
        copy.start()
        self.sent.append(copy)

    def region(self, step, way, block):
        if 2 * step == self.n:
            return self.halves(block)[way]
        return self.whole(block)

    def start(self):
        for way in (0, 1):
            self.go(1, way, self.whole(self.idx))

    def advance(self, step):
        for way in (0, 1):
            came = self.block(step if way else -step)
            self.copy(step, way, self.region(step, way, came)).wait_recv()
            if 2 * step < self.n:
                self.go(step + 1, way, self.region(step + 1, way, came))

    def finish(self):
        for copy in self.sent:
            copy.wait_send()


def picker(offset, transposed):
    shape = (CH, 4 * CH) if transposed else (4 * CH, CH)
    d = lax.broadcasted_iota(jnp.int32, shape, 0 if transposed else 1)
    x = lax.broadcasted_iota(jnp.int32, shape, 1 if transposed else 0)
    return jnp.where(x == (d >> 5) * CH + offset * DIM + (d & 31), 1.0, 0.0).astype(BF)


def node_kernel(
    starting,
    tile_ref,
    mask_smem,
    key_ok_ref,
    w_proj_ref,
    w_bias_ref,
    w_out_ref,
    expand_ref,
    collapse_ref,
    head_ref,
    out_ref,
    nt,
    rows,
    bias,
    k_t,
    v_ext,
    q_exp,
    g_exp,
    gat,
    upd,
    ret,
    a_send,
    a_recv,
    f_send,
    f_recv,
    p_send,
    p_recv,
    g_send,
    g_recv,
    r_send,
    r_recv,
):
    at = here()
    xh, z, xl, y, c = (at[a] for a in AXES)
    x = 2 * xh + xl
    other = 1 - c
    if starting:
        n_peer, take = 8, 6
        me = xl * 4 + y
        peer_place = lambda j, core: place(at, xl=j // 4, y=lax.rem(j, 4), c=core)
        slot = lambda j, core: (2 * j + core, slice(None))
    else:
        n_peer, take = 16, 3
        me = xh * 8 + z
        peer_place = lambda j, core: place(at, xh=j // 8, z=lax.rem(j, 8), c=core)
        slot = lambda j, core: (j, pl.ds(3 * core, 3))

    def peer(d):
        return lax.rem(me + d, n_peer)

    def x_place(step):
        to = lax.rem(x + step + 4, 4)
        return place(at, xh=to // 2, xl=lax.rem(to, 2))

    y_place = lambda step: place(at, y=lax.rem(y + step + 4, 4))
    z_place = lambda step: place(at, z=lax.rem(z + step + 8, 8))
    sibling = place(at, c=other)

    partners = [peer_place(peer(d), c) for d in range(1, n_peer)]
    partners.append(sibling)
    if starting:
        partners += [z_place(d) for d in range(1, 8)]
        far = lax.rem(x + jnp.where(xl == 0, 3, 1), 4)
        partners.append(place(at, xh=far // 2, xl=lax.rem(far, 2)))
    else:
        partners += [peer_place(peer(d), other) for d in range(1, n_peer)]
        partners += [y_place(d) for d in range(1, 4)]
        partners += [x_place(1), x_place(-1)]
    barrier = pltpu.get_barrier_semaphore()
    for partner in partners:
        pl.semaphore_signal(barrier, inc=1, device_id=partner, device_id_type=pl.DeviceIdType.MESH)

    if starting:
        nt[...] = layer_norm(tile_ref[...].astype(F32))
        out_tile = nt
    else:
        out_tile = tile_ref
    own = out_tile[pl.ds(take * me, take)]
    rows[slot(me, c)] = own
    pl.semaphore_wait(barrier, len(partners))

    sends = []
    for d in range(1, n_peer):
        j = peer(d)
        copy = send(
            out_tile.at[pl.ds(take * j, take)],
            rows.at[slot(me, c)],
            a_send.at[d],
            a_recv.at[me],
            peer_place(j, c),
        )
        copy.start()
        sends.append(copy)

    def forward(d):
        j = peer(d)
        region = rows.at[slot(j, c)]
        copy = send(region, region, f_send.at[d], f_recv.at[j], sibling)
        copy.start()
        sends.append(copy)

    forward(0)

    w_all = w_proj_ref[...]
    w_kt = dot(picker(1, True), w_all, NT).astype(BF)
    w_v = dot(w_all, picker(2, False), NN).astype(BF)
    w_qg = jnp.concatenate([dot(w_all, picker(0, False), NN), dot(w_all, picker(3, False), NN)], axis=1).astype(BF)
    s_row = lax.broadcasted_iota(jnp.int32, (24, HEADS), 0)
    s_head = lax.broadcasted_iota(jnp.int32, (24, HEADS), 1)
    w_bias = w_bias_ref[...]
    w_rows = [
        dot(jnp.where(s_row == s_head * ROWS + r, 1.0, 0.0).astype(BF), w_bias, NT).astype(BF) for r in range(ROWS)
    ]

    for d in range(1, n_peer):
        j = peer(d)
        region = rows.at[slot(j, c)]
        send(region, region, a_send.at[d], a_recv.at[j], sibling).wait_recv()
        forward(d)
    for d in range(n_peer):
        j = peer(d)
        region = rows.at[slot(j, other)]
        send(region, region, f_send.at[d], f_recv.at[j], sibling).wait_recv()

    piece = jnp.zeros((24, N), F32)
    for r in range(ROWS):
        piece += dot(w_rows[r], rows[:, r].reshape(N, CH), NT)
    piece = jnp.where(key_ok_ref[...] > 0, piece * ROOT, MASKED)
    if starting:
        source = lax.rem(z, 2) == c
        z4 = z // 2
        own_piece = bias.at[xh, z4, xl, y]
    else:
        source = lax.rem(y, 2) == c
        y2 = y // 2
        own_piece = bias.at[xl, y2, xh, z]

    if starting:
        n_first, line, spot = 8, z, z_place
        part = lambda k: bias.at[xh, k, xl, y]
    else:
        n_first, line, spot = 4, y, y_place
        part = lambda k: bias.at[xl, k, xh, z]

    def first(d):
        return send(own_piece, own_piece, p_send.at[d], p_recv.at[line // 2], spot(d))

    @pl.when(source)
    def _():
        own_piece[...] = piece
        for d in range(1, n_first):
            first(d).start()

    for r in range(ROWS):
        x_r = rows[:, r].reshape(N, CH)
        k_t[r] = dot(w_kt, x_r, NT).astype(BF)
        v_ext[r, :, :CH] = dot(x_r, w_v, NN).astype(BF)
        v_ext[r, :, CH:] = jnp.ones((N, CH), BF)

    for k in range(n_first // 2):

        @pl.when(line != 2 * k + c)
        def _():
            send(part(k), part(k), p_send.at[0], p_recv.at[k], sibling).wait_recv()

    x_args = (x_place(1), x_place(-1), g_send, g_recv)
    if starting:
        y_args = (y_place(1), y_place(-1), g_send, g_recv)
        a1 = Ring(
            4, y, lambda k: bias.at[xh, pl.ds(0, 2), xl, k],
            lambda k: (bias.at[xh, 0, xl, k], bias.at[xh, 1, xl, k]), *y_args, 0,
        )
        b1 = Ring(
            4, x, lambda k: bias.at[k // 2, pl.ds(2, 2), lax.rem(k, 2), y],
            lambda k: (bias.at[k // 2, 2, lax.rem(k, 2), y], bias.at[k // 2, 3, lax.rem(k, 2), y]), *x_args, 8,
        )
        a2 = Ring(
            4, x, lambda k: bias.at[k // 2, pl.ds(0, 2), lax.rem(k, 2)],
            lambda k: (bias.at[k // 2, 0, lax.rem(k, 2)], bias.at[k // 2, 1, lax.rem(k, 2)]), *x_args, 16,
        )
        b2 = Ring(
            4, y, lambda k: bias.at[:, pl.ds(2, 2), :, k],
            lambda k: (bias.at[:, 2, :, k], bias.at[:, 3, :, k]), *y_args, 24,
        )
    else:
        z_args = (z_place(1), z_place(-1), g_send, g_recv)
        a1 = Ring(
            8, z, lambda k: bias.at[xl, 0, xh, k],
            lambda k: (bias.at[xl, 0, xh, k, pl.ds(0, 8)], bias.at[xl, 0, xh, k, pl.ds(8, 16)]), *z_args, 0,
        )
        b1 = Ring(
            4, x, lambda k: bias.at[lax.rem(k, 2), 1, k // 2, z],
            lambda k: (
                bias.at[lax.rem(k, 2), 1, k // 2, z, pl.ds(0, 8)],
                bias.at[lax.rem(k, 2), 1, k // 2, z, pl.ds(8, 16)],
            ), *x_args, 8,
        )
        a2 = Ring(
            4, x, lambda k: bias.at[lax.rem(k, 2), 0, k // 2],
            lambda k: (bias.at[lax.rem(k, 2), 0, k // 2, pl.ds(0, 4)], bias.at[lax.rem(k, 2), 0, k // 2, pl.ds(4, 4)]),
            *x_args, 16,
        )
        b2 = Ring(
            8, z, lambda k: bias.at[:, 1, :, k],
            lambda k: (bias.at[0, 1, :, k], bias.at[1, 1, :, k]), *z_args, 24,
        )

    a1.start()
    b1.start()

    def queries(u):
        if starting:
            spots = (4 * u + c, 4 * u + 2 + c)
        else:
            spots = (4 * u + 2 * c, 4 * u + 2 * c + 1)
        for r in range(ROWS):
            x_q = jnp.concatenate([rows[spots[0], r], rows[spots[1], r]], axis=0)
            qg = dot(x_q, w_qg, NN).astype(BF)
            big = dot(expand_ref[...], qg, NN)
            q_exp[u, r] = (big[:, :CH] * head_ref[...]).astype(BF)
            g_exp[u, r] = jax.nn.sigmoid(big[:, CH:]) * head_ref[...]

    queries(0)
    for step in range(1, 5):
        if 2 * step <= a1.n:
            a1.advance(step)
            if 2 * step == a1.n:
                a2.start()
        if 2 * step <= b1.n:
            b1.advance(step)
            if 2 * step == b1.n:
                b2.start()
    queries(1)
    a2.advance(1)
    b2.advance(1)
    queries(2)
    for step in range(2, 5):
        for ring in (a2, b2):
            if 2 * step <= ring.n:
                ring.advance(step)
        if step == 2:
            queries(3)

    if starting:
        line_at = TILE * (8 * xh + z)
        valid = [mask_smem[line_at + ROWS * me + r] for r in range(ROWS)]
    else:
        line_at = TILE * 2 * (4 * xl + y)
        valid = [mask_smem[line_at + TILE * (r // 3) + 3 * me + r % 3] for r in range(ROWS)]
    power = [v.astype(F32) * (INV_ROOT * LOG2E) for v in valid]
    bias_at = bias.reshape(SUPER, EXP, N)

    @pl.loop(0, SUPER)
    def _(u):
        for r in range(ROWS):
            for s in range(EXP // SUB):
                part = pl.ds(s * SUB, SUB)
                t = dot(q_exp[u, r, part], k_t[r], NN) + bias_at[u, part]
                top = jnp.max(t, axis=1, keepdims=True)
                e = jnp.exp2((t - top) * power[r]).astype(BF)
                o = dot(e, v_ext[r], NN)
                gat[u, r, part] = (g_exp[u, r, part] * (o[:, :CH] / o[:, CH:])).astype(BF)
            both = dot(collapse_ref[...], gat[u, r], NN).astype(BF)
            new = dot(both, w_out_ref[...], NN).astype(BF)
            upd[2 * u, r] = new[:TILE]
            upd[2 * u + 1, r] = new[TILE:]

    if starting:
        for d in range(1, n_peer):
            j = peer(d)
            copy = send(
                upd.at[j], ret.at[pl.ds(take * me, take)], r_send.at[d], r_recv.at[me], peer_place(j, c)
            )
            copy.start()
            sends.append(copy)
        ret[pl.ds(take * me, take)] = upd[me]
        for d in range(1, n_peer):
            j = peer(d)
            region = ret.at[pl.ds(take * j, take)]
            send(region, region, r_send.at[d], r_recv.at[j], sibling).wait_recv()
    else:
        mine = lax.rem(me // 2, 2) == c
        my_q = 2 * (me // 4) + lax.rem(me, 2)
        back = []
        for q in range(8):
            p = 4 * (q // 2) + 2 * c + q % 2
            for core in (0, 1):
                copy = send(
                    upd.at[q, pl.ds(3 * core, 3)],
                    ret.at[pl.ds(take * me, take)],
                    r_send.at[2 * q + core],
                    r_recv.at[me],
                    peer_place(p, core),
                )
                local = jnp.logical_and(p == me, c == core)

                @pl.when(jnp.logical_not(local))
                def _():
                    copy.start()

                back.append((local, copy))

        @pl.when(mine)
        def _():
            ret[pl.ds(take * me, take)] = upd[my_q, pl.ds(3 * c, 3)]

        for d in range(n_peer):
            j = peer(d)
            region = ret.at[pl.ds(take * j, take)]
            come = send(region, region, r_send.at[d], r_recv.at[j], sibling)
            if d == 0:

                @pl.when(jnp.logical_not(mine))
                def _():
                    come.wait_recv()

            else:
                come.wait_recv()
        for local, copy in back:

            @pl.when(jnp.logical_not(local))
            def _():
                copy.wait_send()

    out_ref[...] = ret[...]
    for copy in sends:
        copy.wait_send()

    @pl.when(source)
    def _():
        for d in range(1, n_first):
            first(d).wait_send()

    for ring in (a1, b1, a2, b2):
        ring.finish()


def expansion(starting):
    row = np.arange(EXP)
    if starting:
        blk, slot, r = row // 192, row % 192 // 24, row % 6
        pos = blk * TILE + 6 * slot + r
    else:
        slot, r6 = row // 24, row % 6
        pos = (r6 // 3) * TILE + 3 * slot + r6 % 3
    expand = (pos[:, None] == np.arange(POS)[None, :]).astype(np.float32)
    head = (row // 6 % HEADS)[:, None] == (np.arange(CH) // DIM)[None, :]
    return expand, head.astype(np.float32)


def node(starting, tile, mask, w_proj, w_bias, w_out):
    expand, head = expansion(starting)
    vmem = pl.BlockSpec(memory_space=pltpu.VMEM)
    smem = pl.BlockSpec(memory_space=pltpu.SMEM)
    dma = pltpu.SemaphoreType.DMA
    if starting:
        bias_shape = (2, 4, 2, 4, 24, N)
    else:
        bias_shape = (2, 2, 2, 8, 24, N)
    return pl.pallas_call(
        functools.partial(node_kernel, starting),
        out_shape=jax.ShapeDtypeStruct((TILE, TILE, CH), BF),
        in_specs=[vmem, smem] + [vmem] * 7,
        out_specs=vmem,
        scratch_shapes=[
            pltpu.VMEM((TILE, TILE, CH), BF),
            pltpu.VMEM((16, ROWS, TILE, CH), BF),
            pltpu.VMEM(bias_shape, F32),
            pltpu.VMEM((ROWS, CH, N), BF),
            pltpu.VMEM((ROWS, N, 2 * CH), BF),
            pltpu.VMEM((SUPER, ROWS, EXP, CH), BF),
            pltpu.VMEM((SUPER, ROWS, EXP, CH), F32),
            pltpu.VMEM((SUPER, ROWS, EXP, CH), BF),
            pltpu.VMEM((8, ROWS, TILE, CH), BF),
            pltpu.VMEM((TILE, TILE, CH), BF),
            dma((16,)),
            dma((16,)),
            dma((16,)),
            dma((16,)),
            dma((8,)),
            dma((4,)),
            dma((32,)),
            dma((32,)),
            dma((16,)),
            dma((16,)),
        ],
        compiler_params=pltpu.CompilerParams(
            collective_id=0 if starting else 1, has_side_effects=True, vmem_limit_bytes=56 * 1024 * 1024
        ),
        name="start_node" if starting else "end_node",
    )(
        tile,
        mask,
        mask.reshape(1, N),
        w_proj,
        w_bias,
        w_out,
        jnp.asarray(expand, BF),
        jnp.asarray(expand.T, BF),
        jnp.asarray(head, F32),
    )


def on_device(pair_act, mask, w_proj_start, w_bias_start, w_out_start, w_proj_end, w_bias_end, w_out_end):
    update_start = node(True, pair_act, mask, w_proj_start, w_bias_start, w_out_start)
    updated = pair_act.astype(F32) + update_start.astype(F32)
    flipped = jnp.swapaxes(layer_norm(updated), 0, 1)
    update_end = node(False, flipped, mask, w_proj_end, w_bias_end, w_out_end)
    return update_start, jnp.swapaxes(update_end, 0, 1)


def solution(mesh):
    split = Mesh(mesh.devices.reshape(SIZES), AXES)
    placed = (P(WIDE, NARROW, None),) + (P(),) * 7
    return jax.shard_map(
        on_device,
        mesh=split,
        in_specs=placed,
        out_specs=(P(WIDE, NARROW, None), P(WIDE, NARROW, None)),
        check_vma=False,
    )
```

time: 382 us -> 230 us (0.60)
  Pallas kernels: 0 us -> 216 us
  waiting for transfers between devices: 126 us -> 0 us
  local copies, waits for them, and re-layouts: 82.4 us -> 6.95 us
  blocking collectives: 67.7 us -> 0 us
  matrix products: 42.6 us -> 0 us
  other arithmetic: 29.4 us -> 4.01 us
  starting transfers between devices: 14.6 us -> 0 us
  between operations: 14.5 us -> 0.7 us
    pallas_call x0 -> x2, Pallas kernels: none -> 216 us  [node(): pl.pallas_call(functools.partial(node_kernel, starting), out_shape=jax.Sh...]
    all_to_all x3 -> x0, waiting for transfers between devices: 85.9 us -> none  [the longest x1 52.7 us: on_device(): lax.all_to_all(outgoing_end, 'wide', split_axis=0, concat_axis=2, tiled=T...]
    all_to_all x4 -> x0, blocking collectives: 67.7 us -> none  [the longest x1 27.5 us: on_device(): lax.all_to_all(gated_end.reshape(sub_cols, -1), 'wide', split_axis=1, con...]
    dot_general x54 -> x0, matrix products: 42.6 us -> none  [the longest x24 19.8 us: one_row(): jnp.einsum('hbk,khd->bhd', weights, values, preferred_element_type=jnp.fl...]
    dynamic_slice x73 -> x0, local copies, waits for them, and re-layouts: 40.3 us -> none  [the longest x72 40.2 us: attend(): return lax.map(one_row, (projected, row_ok))]
    all_gather x2 -> x0, waiting for transfers between devices: 39.9 us -> none  [the longest x1 39.9 us: on_device(): pair_bias = lax.all_gather(bias_rows, 'wide', axis=1, tiled=True)]
    all_to_all x12 -> x0, local copies, waits for them, and re-layouts: 15.8 us -> none  [the longest x2 4.44 us: on_device(): lax.all_to_all(gated.reshape(sub_rows, -1), NARROW, split_axis=1, concat_...]
    and x24 -> x0, other arithmetic: 14.6 us -> none  [one_row(): allowed = jnp.logical_and(valid_row, key_ok)]
  transfers between devices with their start and end apart: 5 -> 0, of which waited for: 4 -> 0; matrix products, arithmetic and copies ran while one was open for 4% -> 0% of each run, Pallas kernels for 0% -> 0%
where the time goes in v1:
time: 230 us; the launch traced here: 227 us
  Pallas kernels  216 us (94%)
  local copies, waits for them, and re-layouts  6.95 us (3%)
  other arithmetic  4.01 us (2%)
    pallas_call x2, Pallas kernels, node(): pl.pallas_call(functools.partial(node_kernel, starting), out_shape=jax.Sh...  216 us
    unnamed x8, local copies, waits for them, and re-layouts  5.67 us

profile of v1, /device:TPU:1, one launch (start us, length us, event | category | flops | bytes accessed | tf_op | source)
XLA Modules:
  0.0 227.4 jit_solution(10923732253543107234)
XLA Ops:
  0.6 1.3 reshape.20.key_ok_ref
  1.9 1.4 copy.16.w_bias_ref
  3.3 1.4 copy.19.w_bias_ref
  4.7 0.0 copy-start.1
  4.7 97.0 %start_node.1 = bf16[48,48,128]{2,1,0:T(8,128)(2,1)} custom-call(bf16[48,48,128]{2,1,0:T(8,128)(2,1)} %tile_ref.1, s32[768]{0:T(1024)} %mask_smem.3, s32[1,768]{1,0:T(1,128)} %reshape.20.key_ok_ref, bf16[128,512]{1,0:T(8,128)(2,1)} %w_proj_ref.2, bf16[128,4]{1,0:T(8,128)(2,1)} %copy.16.w_bias_ref, bf16[128,128]{1,0:T(8,128)(2,1)} %w_out_ref.2, ...), custom_call_target="tpu_custom_call" | custom-call | tf_op jit(solution)/shard_map/start_node/pallas_call | solution.py:479
  101.7 0.0 copy-done.1
  101.7 0.0 copy-start
  101.7 1.5 fusion.1
  103.2 0.0 copy-done
  103.3 0.7 multiply_reduce_fusion
  104.0 1.8 fusion.2.tile_ref
  105.8 118.8 %end_node.1 = bf16[48,48,128]{2,1,0:T(8,128)(2,1)} custom-call(bf16[48,48,128]{2,1,0:T(8,128)(2,1)} %fusion.2.tile_ref, s32[768]{0:T(1024)} %mask_smem.3, s32[1,768]{1,0:T(1,128)} %reshape.20.key_ok_ref, bf16[128,512]{1,0:T(8,128)(2,1)} %w_proj_ref.3, bf16[128,4]{1,0:T(8,128)(2,1)} %copy.19.w_bias_ref, bf16[128,128]{1,0:T(8,128)(2,1)} %w_out_ref.3, ...), custom_call_target="tpu_custom_call" | custom-call | tf_op jit(solution)/shard_map/end_node/pallas_call | solution.py:479
  224.5 2.0 copy.20
  226.6 0.8 copy.28
  (2 shorter events, 0.0 us)
Async XLA Ops:
  4.7 97.0 %copy-start.1 = (bf16[48,48,128]{2,1,0:T(8,128)(2,1)S(1)}, bf16[48,48,128]{2,1,0:T(8,128)(2,1)}, u32[]{:S(2)}) copy-start(bf16[48,48,128]{2,1,0:T(8,128)(2,1)} %tile_ref.1) | copy-start | bytes 1769476
  101.7 1.5 copy-start

commit v2 on v1

--- a/solution.py
+++ b/solution.py
@@ -69,44 +69,46 @@
 
 
 class Ring:
-    def __init__(self, n, idx, whole, halves, plus, minus, ssem, rsem, base):
-        self.n, self.idx = n, idx
+    def __init__(self, n, idx, whole, halves, plus, minus, ssem, rsem, base, has=None):
+        self.n, self.idx, self.has = n, idx, has
         self.whole, self.halves = whole, halves
         self.plus, self.minus = plus, minus
         self.ssem, self.rsem, self.base = ssem, rsem, base
-        self.sent = []
 
     def block(self, offset):
         return lax.rem(self.idx + offset + self.n, self.n)
 
-    def copy(self, step, way, region):
+    def copy(self, step, way, block):
+        region = self.halves(block)[way] if 2 * step == self.n else self.whole(block)
         at = self.base + 2 * (step - 1) + way
         return send(region, region, self.ssem.at[at], self.rsem.at[at], self.minus if way else self.plus)
 
-    def go(self, step, way, region):
-        copy = self.copy(step, way, region)
-        copy.start()
-        self.sent.append(copy)
-
-    def region(self, step, way, block):
-        if 2 * step == self.n:
-            return self.halves(block)[way]
-        return self.whole(block)
+    def where(self, block, do):
+        if self.has is None:
+            do()
+        else:
+            pl.when(self.has(block))(do)
 
     def start(self):
         for way in (0, 1):
-            self.go(1, way, self.whole(self.idx))
+            self.where(self.idx, lambda: self.copy(1, way, self.idx).start())
 
     def advance(self, step):
         for way in (0, 1):
             came = self.block(step if way else -step)
-            self.copy(step, way, self.region(step, way, came)).wait_recv()
-            if 2 * step < self.n:
-                self.go(step + 1, way, self.region(step + 1, way, came))
+
+            def do():
+                self.copy(step, way, came).wait_recv()
+                if 2 * step < self.n:
+                    self.copy(step + 1, way, came).start()
+
+            self.where(came, do)
 
     def finish(self):
-        for copy in self.sent:
-            copy.wait_send()
+        for step in range(1, self.n // 2 + 1):
+            for way in (0, 1):
+                block = self.block(step - 1 if way else 1 - step)
+                self.where(block, lambda: self.copy(step, way, block).wait_send())
 
 
 def picker(offset, transposed):
@@ -245,29 +247,25 @@
     for r in range(ROWS):
         piece += dot(w_rows[r], rows[:, r].reshape(N, CH), NT)
     piece = jnp.where(key_ok_ref[...] > 0, piece * ROOT, MASKED)
+    y2 = y // 2
     if starting:
         source = lax.rem(z, 2) == c
-        z4 = z // 2
-        own_piece = bias.at[xh, z4, xl, y]
+        own_piece = bias.at[xh, z // 2, xl, y]
+        part = lambda k: bias.at[xh, k // 2, xl, y]
+        comes = lambda k: jnp.logical_and(lax.rem(k, 2) == c, k != z)
     else:
         source = lax.rem(y, 2) == c
-        y2 = y // 2
         own_piece = bias.at[xl, y2, xh, z]
-
-    if starting:
-        n_first, line, spot = 8, z, z_place
-        part = lambda k: bias.at[xh, k, xl, y]
-    else:
-        n_first, line, spot = 4, y, y_place
-        part = lambda k: bias.at[xl, k, xh, z]
+        part = lambda k: bias.at[xl, y2, xh, k]
+        comes = lambda k: jnp.logical_and(source, k != z)
 
     def first(d):
-        return send(own_piece, own_piece, p_send.at[d], p_recv.at[line // 2], spot(d))
+        return send(own_piece, own_piece, p_send.at[d], p_recv.at[z], z_place(d))
 
     @pl.when(source)
     def _():
         own_piece[...] = piece
-        for d in range(1, n_first):
+        for d in range(1, 8):
             first(d).start()
 
     for r in range(ROWS):
@@ -276,89 +274,93 @@
         v_ext[r, :, :CH] = dot(x_r, w_v, NN).astype(BF)
         v_ext[r, :, CH:] = jnp.ones((N, CH), BF)
 
-    for k in range(n_first // 2):
-
-        @pl.when(line != 2 * k + c)
-        def _():
-            send(part(k), part(k), p_send.at[0], p_recv.at[k], sibling).wait_recv()
-
-    x_args = (x_place(1), x_place(-1), g_send, g_recv)
-    if starting:
-        y_args = (y_place(1), y_place(-1), g_send, g_recv)
-        a1 = Ring(
-            4, y, lambda k: bias.at[xh, pl.ds(0, 2), xl, k],
-            lambda k: (bias.at[xh, 0, xl, k], bias.at[xh, 1, xl, k]), *y_args, 0,
-        )
-        b1 = Ring(
-            4, x, lambda k: bias.at[k // 2, pl.ds(2, 2), lax.rem(k, 2), y],
-            lambda k: (bias.at[k // 2, 2, lax.rem(k, 2), y], bias.at[k // 2, 3, lax.rem(k, 2), y]), *x_args, 8,
-        )
-        a2 = Ring(
-            4, x, lambda k: bias.at[k // 2, pl.ds(0, 2), lax.rem(k, 2)],
-            lambda k: (bias.at[k // 2, 0, lax.rem(k, 2)], bias.at[k // 2, 1, lax.rem(k, 2)]), *x_args, 16,
-        )
-        b2 = Ring(
-            4, y, lambda k: bias.at[:, pl.ds(2, 2), :, k],
-            lambda k: (bias.at[:, 2, :, k], bias.at[:, 3, :, k]), *y_args, 24,
-        )
-    else:
-        z_args = (z_place(1), z_place(-1), g_send, g_recv)
-        a1 = Ring(
-            8, z, lambda k: bias.at[xl, 0, xh, k],
-            lambda k: (bias.at[xl, 0, xh, k, pl.ds(0, 8)], bias.at[xl, 0, xh, k, pl.ds(8, 16)]), *z_args, 0,
-        )
-        b1 = Ring(
-            4, x, lambda k: bias.at[lax.rem(k, 2), 1, k // 2, z],
-            lambda k: (
-                bias.at[lax.rem(k, 2), 1, k // 2, z, pl.ds(0, 8)],
-                bias.at[lax.rem(k, 2), 1, k // 2, z, pl.ds(8, 16)],
-            ), *x_args, 8,
-        )
-        a2 = Ring(
-            4, x, lambda k: bias.at[lax.rem(k, 2), 0, k // 2],
-            lambda k: (bias.at[lax.rem(k, 2), 0, k // 2, pl.ds(0, 4)], bias.at[lax.rem(k, 2), 0, k // 2, pl.ds(4, 4)]),
-            *x_args, 16,
-        )
-        b2 = Ring(
-            8, z, lambda k: bias.at[:, 1, :, k],
-            lambda k: (bias.at[0, 1, :, k], bias.at[1, 1, :, k]), *z_args, 24,
-        )
-
-    a1.start()
-    b1.start()
-
-    def queries(u):
+    def queries(u, r):
         if starting:
             spots = (4 * u + c, 4 * u + 2 + c)
         else:
             spots = (4 * u + 2 * c, 4 * u + 2 * c + 1)
-        for r in range(ROWS):
-            x_q = jnp.concatenate([rows[spots[0], r], rows[spots[1], r]], axis=0)
-            qg = dot(x_q, w_qg, NN).astype(BF)
-            big = dot(expand_ref[...], qg, NN)
-            q_exp[u, r] = (big[:, :CH] * head_ref[...]).astype(BF)
-            g_exp[u, r] = jax.nn.sigmoid(big[:, CH:]) * head_ref[...]
-
-    queries(0)
-    for step in range(1, 5):
-        if 2 * step <= a1.n:
-            a1.advance(step)
-            if 2 * step == a1.n:
-                a2.start()
-        if 2 * step <= b1.n:
-            b1.advance(step)
-            if 2 * step == b1.n:
-                b2.start()
-    queries(1)
-    a2.advance(1)
-    b2.advance(1)
-    queries(2)
-    for step in range(2, 5):
-        for ring in (a2, b2):
-            if 2 * step <= ring.n:
-                ring.advance(step)
-        if step == 2:
-            queries(3)
+        x_q = jnp.concatenate([rows[spots[0], r], rows[spots[1], r]], axis=0)
+        qg = dot(x_q, w_qg, NN).astype(BF)
+        big = dot(expand_ref[...], qg, NN)
+        q = (big[:, :CH] * head_ref[...]).reshape(*lead, 24, CH)
+        g = (jax.nn.sigmoid(big[:, CH:]) * head_ref[...]).reshape(*lead, 24, CH)
+        q_exp[(r, *in_super(u))] = q
+        g_exp[(r, *in_super(u))] = g
+
+    if starting:
+        lead = (2, 2, 4)
+        in_super = lambda u: (u // 2, pl.ds(2 * (u % 2), 2))
+    else:
+        lead = (2, 8)
+        in_super = lambda u: (u // 2, u % 2)
+
+    for r in range(ROWS):
+        queries(0, r)
+        queries(1, r)
+
+    for k in range(8):
+
+        @pl.when(comes(k))
+        def _():
+            send(part(k), part(k), p_send.at[0], p_recv.at[k], sibling).wait_recv()
+
+    x_args = (x_place(1), x_place(-1), g_send, g_recv)
+    y_args = (y_place(1), y_place(-1), g_send, g_recv)
+    if starting:
+        a1 = Ring(
+            4, y, lambda k: bias.at[xh, pl.ds(0, 2), xl, k],
+            lambda k: (bias.at[xh, 0, xl, k], bias.at[xh, 1, xl, k]), *y_args, 0,
+        )
+        b1 = Ring(
+            4, x, lambda k: bias.at[k // 2, pl.ds(2, 2), lax.rem(k, 2), y],
+            lambda k: (bias.at[k // 2, 2, lax.rem(k, 2), y], bias.at[k // 2, 3, lax.rem(k, 2), y]), *x_args, 4,
+        )
+        a2 = Ring(
+            4, x, lambda k: bias.at[k // 2, pl.ds(0, 2), lax.rem(k, 2)],
+            lambda k: (bias.at[k // 2, 0, lax.rem(k, 2)], bias.at[k // 2, 1, lax.rem(k, 2)]), *x_args, 8,
+        )
+        b2 = Ring(
+            4, y, lambda k: bias.at[:, pl.ds(2, 2), :, k],
+            lambda k: (bias.at[:, 2, :, k], bias.at[:, 3, :, k]), *y_args, 12,
+        )
+    else:
+        has = lambda k: lax.rem(k, 2) == c
+        here_only = lambda k: source
+        a1 = Ring(
+            4, y, lambda k: bias.at[xl, k // 2, xh, pl.ds(0, 4)],
+            lambda k: (bias.at[xl, k // 2, xh, pl.ds(0, 2)], bias.at[xl, k // 2, xh, pl.ds(2, 2)]), *y_args, 0, has,
+        )
+        b1 = Ring(
+            4, x, lambda k: bias.at[lax.rem(k, 2), y2, k // 2, pl.ds(4, 4)],
+            lambda k: (
+                bias.at[lax.rem(k, 2), y2, k // 2, pl.ds(4, 2)],
+                bias.at[lax.rem(k, 2), y2, k // 2, pl.ds(6, 2)],
+            ), *x_args, 4, here_only,
+        )
+        a2 = Ring(
+            4, x, lambda k: bias.at[lax.rem(k, 2), :, k // 2, pl.ds(0, 4)],
+            lambda k: (
+                bias.at[lax.rem(k, 2), 0, k // 2, pl.ds(0, 4)],
+                bias.at[lax.rem(k, 2), 1, k // 2, pl.ds(0, 4)],
+            ), *x_args, 8,
+        )
+        b2 = Ring(
+            4, y, lambda k: bias.at[:, k // 2, :, pl.ds(4, 4)],
+            lambda k: (bias.at[0, k // 2, :, pl.ds(4, 4)], bias.at[1, k // 2, :, pl.ds(4, 4)]), *y_args, 12, has,
+        )
+
+    a1.start()
+    b1.start()
+    for r in range(ROWS):
+        queries(2, r)
+    a1.advance(1)
+    b1.advance(1)
+    for r in range(ROWS):
+        queries(3, r)
+    a1.advance(2)
+    b1.advance(2)
+    a2.start()
+    b2.start()
 
     if starting:
         line_at = TILE * (8 * xh + z)
@@ -367,19 +369,56 @@
         line_at = TILE * 2 * (4 * xl + y)
         valid = [mask_smem[line_at + TILE * (r // 3) + 3 * me + r % 3] for r in range(ROWS)]
     power = [v.astype(F32) * (INV_ROOT * LOG2E) for v in valid]
-    bias_at = bias.reshape(SUPER, EXP, N)
-
-    @pl.loop(0, SUPER)
-    def _(u):
+
+    def attend(at):
+        pairs = bias[at].reshape(SUB, N)
         for r in range(ROWS):
-            for s in range(EXP // SUB):
-                part = pl.ds(s * SUB, SUB)
-                t = dot(q_exp[u, r, part], k_t[r], NN) + bias_at[u, part]
-                top = jnp.max(t, axis=1, keepdims=True)
-                e = jnp.exp2((t - top) * power[r]).astype(BF)
-                o = dot(e, v_ext[r], NN)
-                gat[u, r, part] = (g_exp[u, r, part] * (o[:, :CH] / o[:, CH:])).astype(BF)
-            both = dot(collapse_ref[...], gat[u, r], NN).astype(BF)
+            t = dot(q_exp[(r, *at)].reshape(SUB, CH).astype(BF), k_t[r], NN) + pairs
+            top = jnp.max(t, axis=1, keepdims=True)
+            e = jnp.exp2((t - top) * power[r]).astype(BF)
+            o = dot(e, v_ext[r], NN)
+            gated = g_exp[(r, *at)].reshape(SUB, CH) * (o[:, :CH] / o[:, CH:])
+            gat[(r, *at)] = gated.reshape(*q_exp[(r, *at)].shape)
+
+    @pl.loop(0, 4)
+    def _(t):
+        step = jnp.where(t == 3, 2, jnp.where(t == 2, 3, t))
+
+        @pl.when(t == 1)
+        def _():
+            a2.advance(1)
+            if starting:
+                b2.advance(1)
+
+        @pl.when(t == 2)
+        def _():
+            if not starting:
+                b2.advance(2)
+
+        @pl.when(t == 3)
+        def _():
+            a2.advance(2)
+            if starting:
+                b2.advance(2)
+
+        xc = lax.rem(x + step, 4)
+        if starting:
+            attend((xc // 2, pl.ds(0, 2), lax.rem(xc, 2)))
+            attend((slice(None), pl.ds(2, 2), slice(None), lax.rem(y + step, 4)))
+        else:
+            attend((lax.rem(xc, 2), slice(None), xc // 2, pl.ds(0, 4)))
+
+            @pl.when(t == 0)
+            def _():
+                b2.advance(1)
+
+            y_c = jnp.where(t < 2, y2, 1 - y2)
+            attend((lax.rem(t, 2), y_c, slice(None), pl.ds(4, 4)))
+
+    for u in range(SUPER):
+        for r in range(ROWS):
+            wide = gat[(r, *in_super(u))].reshape(EXP, CH).astype(BF)
+            both = dot(collapse_ref[...], wide, NN).astype(BF)
             new = dot(both, w_out_ref[...], NN).astype(BF)
             upd[2 * u, r] = new[:TILE]
             upd[2 * u + 1, r] = new[TILE:]
@@ -447,7 +486,7 @@
 
     @pl.when(source)
     def _():
-        for d in range(1, n_first):
+        for d in range(1, 8):
             first(d).wait_send()
 
     for ring in (a1, b1, a2, b2):
@@ -487,9 +526,9 @@
             pltpu.VMEM(bias_shape, F32),
             pltpu.VMEM((ROWS, CH, N), BF),
             pltpu.VMEM((ROWS, N, 2 * CH), BF),
-            pltpu.VMEM((SUPER, ROWS, EXP, CH), BF),
-            pltpu.VMEM((SUPER, ROWS, EXP, CH), F32),
-            pltpu.VMEM((SUPER, ROWS, EXP, CH), BF),
+            pltpu.VMEM((ROWS, *bias_shape[:-1], CH), F32),
+            pltpu.VMEM((ROWS, *bias_shape[:-1], CH), F32),
+            pltpu.VMEM((ROWS, *bias_shape[:-1], CH), F32),
             pltpu.VMEM((8, ROWS, TILE, CH), BF),
             pltpu.VMEM((TILE, TILE, CH), BF),
             dma((16,)),
@@ -497,9 +536,9 @@
             dma((16,)),
             dma((16,)),
             dma((8,)),
-            dma((4,)),
-            dma((32,)),
-            dma((32,)),
+            dma((8,)),
+            dma((16,)),
+            dma((16,)),
             dma((16,)),
             dma((16,)),
         ],

time: 230 us -> 189 us (0.82); the launches traced: 227 us -> 189 us
  Pallas kernels: 216 us -> 177 us
    pallas_call x2, Pallas kernels: 216 us -> 177 us  [node(): pl.pallas_call(functools.partial(node_kernel, starting), out_shape=jax.Sh...]
where the time goes in v2:
time: 189 us
  Pallas kernels  177 us (94%)
  local copies, waits for them, and re-layouts  6.95 us (4%)
  other arithmetic  4.01 us (2%)
    pallas_call x2, Pallas kernels, node(): pl.pallas_call(functools.partial(node_kernel, starting), out_shape=jax.Sh...  177 us
    unnamed x8, local copies, waits for them, and re-layouts  5.67 us

profile of v2, /device:TPU:1, one launch (start us, length us, event | category | flops | bytes accessed | tf_op | source)
XLA Modules:
  0.0 189.1 jit_solution(12322851204458868454)
XLA Ops:
  0.6 1.3 reshape.20.key_ok_ref
  1.9 1.4 copy.16.w_bias_ref
  3.3 1.4 copy.19.w_bias_ref
  4.7 0.0 copy-start.1
  4.7 77.8 %start_node.1 = bf16[48,48,128]{2,1,0:T(8,128)(2,1)} custom-call(bf16[48,48,128]{2,1,0:T(8,128)(2,1)} %tile_ref.1, s32[768]{0:T(1024)} %mask_smem.3, s32[1,768]{1,0:T(1,128)} %reshape.20.key_ok_ref, bf16[128,512]{1,0:T(8,128)(2,1)} %w_proj_ref.2, bf16[128,4]{1,0:T(8,128)(2,1)} %copy.16.w_bias_ref, bf16[128,128]{1,0:T(8,128)(2,1)} %w_out_ref.2, ...), custom_call_target="tpu_custom_call" | custom-call | tf_op jit(solution)/shard_map/start_node/pallas_call | solution.py:518
  82.5 0.0 copy-done.1
  82.5 0.0 copy-start
  82.5 1.5 fusion.1
  84.0 0.0 copy-done
  84.1 0.7 multiply_reduce_fusion
  84.8 1.8 fusion.2.tile_ref
  86.6 99.7 %end_node.1 = bf16[48,48,128]{2,1,0:T(8,128)(2,1)} custom-call(bf16[48,48,128]{2,1,0:T(8,128)(2,1)} %fusion.2.tile_ref, s32[768]{0:T(1024)} %mask_smem.3, s32[1,768]{1,0:T(1,128)} %reshape.20.key_ok_ref, bf16[128,512]{1,0:T(8,128)(2,1)} %w_proj_ref.3, bf16[128,4]{1,0:T(8,128)(2,1)} %copy.19.w_bias_ref, bf16[128,128]{1,0:T(8,128)(2,1)} %w_out_ref.3, ...), custom_call_target="tpu_custom_call" | custom-call | tf_op jit(solution)/shard_map/end_node/pallas_call | solution.py:518
  186.2 2.0 %copy.20 = bf16[48,48,128]{2,1,0:T(8,128)(2,1)} copy(bf16[48,48,128]{2,0,1:T(8,128)(2,1)} %bitcast.3) | data formatting | bytes 1179648
  188.3 0.8 copy.28
  (2 shorter events, 0.0 us)
Async XLA Ops:
  4.7 77.8 %copy-start.1 = (bf16[48,48,128]{2,1,0:T(8,128)(2,1)S(1)}, bf16[48,48,128]{2,1,0:T(8,128)(2,1)}, u32[]{:S(2)}) copy-start(bf16[48,48,128]{2,1,0:T(8,128)(2,1)} %tile_ref.1) | copy-start | bytes 1769476
  82.5 1.5 copy-start

commit v3 on v2

--- a/solution.py
+++ b/solution.py
@@ -118,39 +118,11 @@
     return jnp.where(x == (d >> 5) * CH + offset * DIM + (d & 31), 1.0, 0.0).astype(BF)
 
 
-def node_kernel(
-    starting,
-    tile_ref,
-    mask_smem,
-    key_ok_ref,
-    w_proj_ref,
-    w_bias_ref,
-    w_out_ref,
-    expand_ref,
-    collapse_ref,
-    head_ref,
-    out_ref,
-    nt,
-    rows,
-    bias,
-    k_t,
-    v_ext,
-    q_exp,
-    g_exp,
-    gat,
-    upd,
-    ret,
-    a_send,
-    a_recv,
-    f_send,
-    f_recv,
-    p_send,
-    p_recv,
-    g_send,
-    g_recv,
-    r_send,
-    r_recv,
-):
+def run(starting, b, barrier_done, out_tile, rows, bias, ret, sems):
+    mask_smem, key_ok, w_proj_ref, w_bias_ref, w_out_ref, expand_ref, collapse_ref, head_ref = b.given[starting]
+    k_t, v_ext, upd = b.k_t, b.v_ext, b.upd
+    q_exp, g_exp, gat = (ref.reshape(ROWS, *bias.shape[:-1], CH) for ref in (b.q_exp, b.g_exp, b.gat))
+    a_send, a_recv, f_send, f_recv, p_send, p_recv, g_send, g_recv, r_send, r_recv = sems
     at = here()
     xh, z, xl, y, c = (at[a] for a in AXES)
     x = 2 * xh + xl
@@ -177,28 +149,9 @@
     z_place = lambda step: place(at, z=lax.rem(z + step + 8, 8))
     sibling = place(at, c=other)
 
-    partners = [peer_place(peer(d), c) for d in range(1, n_peer)]
-    partners.append(sibling)
-    if starting:
-        partners += [z_place(d) for d in range(1, 8)]
-        far = lax.rem(x + jnp.where(xl == 0, 3, 1), 4)
-        partners.append(place(at, xh=far // 2, xl=lax.rem(far, 2)))
-    else:
-        partners += [peer_place(peer(d), other) for d in range(1, n_peer)]
-        partners += [y_place(d) for d in range(1, 4)]
-        partners += [x_place(1), x_place(-1)]
-    barrier = pltpu.get_barrier_semaphore()
-    for partner in partners:
-        pl.semaphore_signal(barrier, inc=1, device_id=partner, device_id_type=pl.DeviceIdType.MESH)
-
-    if starting:
-        nt[...] = layer_norm(tile_ref[...].astype(F32))
-        out_tile = nt
-    else:
-        out_tile = tile_ref
     own = out_tile[pl.ds(take * me, take)]
     rows[slot(me, c)] = own
-    pl.semaphore_wait(barrier, len(partners))
+    barrier_done()
 
     sends = []
     for d in range(1, n_peer):
@@ -230,7 +183,7 @@
     s_head = lax.broadcasted_iota(jnp.int32, (24, HEADS), 1)
     w_bias = w_bias_ref[...]
     w_rows = [
-        dot(jnp.where(s_row == s_head * ROWS + r, 1.0, 0.0).astype(BF), w_bias, NT).astype(BF) for r in range(ROWS)
+        dot(jnp.where(s_row == s_head * ROWS + r, 1.0, 0.0).astype(BF), w_bias, NN).astype(BF) for r in range(ROWS)
     ]
 
     for d in range(1, n_peer):
@@ -246,7 +199,7 @@
     piece = jnp.zeros((24, N), F32)
     for r in range(ROWS):
         piece += dot(w_rows[r], rows[:, r].reshape(N, CH), NT)
-    piece = jnp.where(key_ok_ref[...] > 0, piece * ROOT, MASKED)
+    piece = jnp.where(key_ok > 0, piece * ROOT, MASKED)
     y2 = y // 2
     if starting:
         source = lax.rem(z, 2) == c
@@ -480,17 +433,98 @@
             def _():
                 copy.wait_send()
 
-    out_ref[...] = ret[...]
-    for copy in sends:
-        copy.wait_send()
-
-    @pl.when(source)
-    def _():
-        for d in range(1, 8):
-            first(d).wait_send()
-
-    for ring in (a1, b1, a2, b2):
-        ring.finish()
+    def finish():
+        for copy in sends:
+            copy.wait_send()
+
+        @pl.when(source)
+        def _():
+            for d in range(1, 8):
+                first(d).wait_send()
+
+        for ring in (a1, b1, a2, b2):
+            ring.finish()
+
+    return finish
+
+
+class Bag:
+    pass
+
+
+def kernel(
+    tile_ref,
+    mask_smem,
+    mask_ref,
+    ps_ref,
+    bs_ref,
+    os_ref,
+    pe_ref,
+    be_ref,
+    oe_ref,
+    es_ref,
+    cs_ref,
+    ee_ref,
+    ce_ref,
+    head_ref,
+    start_ref,
+    end_ref,
+    nt_start,
+    nt_end,
+    rows_start,
+    rows_end,
+    bias_start,
+    bias_end,
+    ret_start,
+    ret_end,
+    k_t,
+    v_ext,
+    q_exp,
+    g_exp,
+    gat,
+    upd,
+    *sems,
+):
+    at = here()
+    xh, z, xl, y, c = (at[a] for a in AXES)
+    x = 2 * xh + xl
+    narrow_me, wide_me = xl * 4 + y, xh * 8 + z
+    partners = [place(at, c=1 - c)]
+    for d in range(1, 8):
+        j = lax.rem(narrow_me + d, 8)
+        partners.append(place(at, xl=j // 4, y=lax.rem(j, 4)))
+    for d in range(1, 16):
+        j = lax.rem(wide_me + d, 16)
+        for core in (c, 1 - c):
+            partners.append(place(at, xh=j // 8, z=lax.rem(j, 8), c=core))
+    far = lax.rem(x + jnp.where(xl == 0, 3, 1), 4)
+    partners.append(place(at, xh=far // 2, xl=lax.rem(far, 2)))
+    barrier = pltpu.get_barrier_semaphore()
+    for partner in partners:
+        pl.semaphore_signal(barrier, inc=1, device_id=partner, device_id_type=pl.DeviceIdType.MESH)
+
+    b = Bag()
+    b.k_t, b.v_ext, b.upd = k_t, v_ext, upd
+    b.q_exp, b.g_exp, b.gat = q_exp, g_exp, gat
+    key_ok = mask_ref[...].reshape(1, N)
+    b.given = {
+        True: (mask_smem, key_ok, ps_ref, bs_ref, os_ref, es_ref, cs_ref, head_ref),
+        False: (mask_smem, key_ok, pe_ref, be_ref, oe_ref, ee_ref, ce_ref, head_ref),
+    }
+    half = len(sems) // 2
+
+    nt_start[...] = layer_norm(tile_ref[...].astype(F32))
+    finish_start = run(
+        True, b, lambda: pl.semaphore_wait(barrier, len(partners)), nt_start, rows_start, bias_start, ret_start, sems[:half]
+    )
+    update = ret_start[...]
+    start_ref[...] = update
+    normed = layer_norm(tile_ref[...].astype(F32) + update.astype(F32))
+    nt_end[...] = jnp.swapaxes(normed.astype(F32), 0, 1).astype(BF)
+    finish_start()
+    finish_end = run(False, b, lambda: None, nt_end, rows_end, bias_end, ret_end, sems[half:])
+    end_ref[...] = jnp.swapaxes(ret_end[...].astype(F32), 0, 1).astype(BF)
+    finish_end()
 
 
 def expansion(starting):
@@ -506,65 +540,58 @@
     return expand, head.astype(np.float32)
 
 
-def node(starting, tile, mask, w_proj, w_bias, w_out):
-    expand, head = expansion(starting)
+def on_device(pair_act, mask, w_proj_start, w_bias_start, w_out_start, w_proj_end, w_bias_end, w_out_end):
+    (e_start, head), (e_end, _) = expansion(True), expansion(False)
     vmem = pl.BlockSpec(memory_space=pltpu.VMEM)
     smem = pl.BlockSpec(memory_space=pltpu.SMEM)
     dma = pltpu.SemaphoreType.DMA
-    if starting:
-        bias_shape = (2, 4, 2, 4, 24, N)
-    else:
-        bias_shape = (2, 2, 2, 8, 24, N)
+    tile = pltpu.VMEM((TILE, TILE, CH), BF)
+    rows = pltpu.VMEM((16, ROWS, TILE, CH), BF)
+    wide_rows = pltpu.VMEM((ROWS, 64, 24, CH), F32)
+    sems = [dma((16,)) for _ in range(4)] + [dma((8,)) for _ in range(2)] + [dma((16,)) for _ in range(4)]
     return pl.pallas_call(
-        functools.partial(node_kernel, starting),
-        out_shape=jax.ShapeDtypeStruct((TILE, TILE, CH), BF),
-        in_specs=[vmem, smem] + [vmem] * 7,
-        out_specs=vmem,
+        kernel,
+        out_shape=[jax.ShapeDtypeStruct((TILE, TILE, CH), BF)] * 2,
+        in_specs=[vmem, smem] + [vmem] * 12,
+        out_specs=[vmem, vmem],
         scratch_shapes=[
-            pltpu.VMEM((TILE, TILE, CH), BF),
-            pltpu.VMEM((16, ROWS, TILE, CH), BF),
-            pltpu.VMEM(bias_shape, F32),
+            tile,
+            tile,
+            rows,
+            rows,
+            pltpu.VMEM((2, 4, 2, 4, 24, N), F32),
+            pltpu.VMEM((2, 2, 2, 8, 24, N), F32),
+            tile,
+            tile,
             pltpu.VMEM((ROWS, CH, N), BF),
             pltpu.VMEM((ROWS, N, 2 * CH), BF),
-            pltpu.VMEM((ROWS, *bias_shape[:-1], CH), F32),
-            pltpu.VMEM((ROWS, *bias_shape[:-1], CH), F32),
-            pltpu.VMEM((ROWS, *bias_shape[:-1], CH), F32),
+            wide_rows,
+            wide_rows,
+            wide_rows,
             pltpu.VMEM((8, ROWS, TILE, CH), BF),
-            pltpu.VMEM((TILE, TILE, CH), BF),
-            dma((16,)),
-            dma((16,)),
-            dma((16,)),
-            dma((16,)),
-            dma((8,)),
-            dma((8,)),
-            dma((16,)),
-            dma((16,)),
-            dma((16,)),
-            dma((16,)),
-        ],
+        ]
+        + sems
+        + sems,
         compiler_params=pltpu.CompilerParams(
-            collective_id=0 if starting else 1, has_side_effects=True, vmem_limit_bytes=56 * 1024 * 1024
+            collective_id=0, has_side_effects=True, vmem_limit_bytes=56 * 1024 * 1024
         ),
-        name="start_node" if starting else "end_node",
+        name="triangle_attention",
     )(
-        tile,
+        pair_act,
         mask,
-        mask.reshape(1, N),
-        w_proj,
-        w_bias,
-        w_out,
-        jnp.asarray(expand, BF),
-        jnp.asarray(expand.T, BF),
+        mask,
+        w_proj_start,
+        w_bias_start.T,
+        w_out_start,
+        w_proj_end,
+        w_bias_end.T,
+        w_out_end,
+        jnp.asarray(e_start, BF),
+        jnp.asarray(e_start.T, BF),
+        jnp.asarray(e_end, BF),
+        jnp.asarray(e_end.T, BF),
         jnp.asarray(head, F32),
     )
-
-
-def on_device(pair_act, mask, w_proj_start, w_bias_start, w_out_start, w_proj_end, w_bias_end, w_out_end):
-    update_start = node(True, pair_act, mask, w_proj_start, w_bias_start, w_out_start)
-    updated = pair_act.astype(F32) + update_start.astype(F32)
-    flipped = jnp.swapaxes(layer_norm(updated), 0, 1)
-    update_end = node(False, flipped, mask, w_proj_end, w_bias_end, w_out_end)
-    return update_start, jnp.swapaxes(update_end, 0, 1)
 
 
 def solution(mesh):

time: 189 us -> 170 us (0.90)
  Pallas kernels: 177 us -> 166 us
  local copies, waits for them, and re-layouts: 6.95 us -> 2.8 us
  other arithmetic: 4.01 us -> 0 us
    pallas_call x2 -> x1, Pallas kernels: 177 us -> 166 us  [on_device(): pl.pallas_call(kernel, out_shape=[jax.ShapeDtypeStruct((TILE, TILE, CH),...]
    unnamed x8 -> x4, local copies, waits for them, and re-layouts: 5.67 us -> 2.8 us
    reduce_sum x2 -> x0, other arithmetic: 2.23 us -> none  [the longest x1 1.51 us: layer_norm(): average = jnp.mean(features, axis=-1, keepdims=True)]
where the time goes in v3:
time: 170 us; the launch traced here: 169 us
  Pallas kernels  166 us (98%)
  local copies, waits for them, and re-layouts  2.8 us (2%)
    pallas_call x1, Pallas kernels, on_device(): pl.pallas_call(kernel, out_shape=[jax.ShapeDtypeStruct((TILE, TILE, CH),...  166 us

profile of v3, /device:TPU:1, one launch (start us, length us, event | category | flops | bytes accessed | tf_op | source)
XLA Modules:
  0.0 169.3 jit_solution(15069571600567995172)
XLA Ops:
  0.6 165.9 %triangle_attention.1 = (bf16[48,48,128]{2,1,0:T(8,128)(2,1)}, bf16[48,48,128]{2,1,0:T(8,128)(2,1)}) custom-call(bf16[48,48,128]{2,1,0:T(8,128)(2,1)} %tile_ref.1, s32[768]{0:T(1024)} %mask_ref.1, s32[768]{0:T(1024)} %mask_ref.1, bf16[128,512]{1,0:T(8,128)(2,1)} %ps_ref.1, bf16[4,128]{1,0:T(4,128)(2,1)} %bitcast.2, bf16[128,128]{1,0:T(8,128)(2,1)} %os_ref.1, ...), custom_call_target="tpu_custom_call" | custom-call | tf_op jit(solution)/shard_map/triangle_attention/pallas_call | solution.py:552
  166.5 0.0 copy-start
  166.5 2.0 %copy.17 = bf16[48,48,128]{2,1,0:T(8,128)(2,1)} copy(bf16[48,48,128]{2,1,0:T(8,128)(2,1)} %get-tuple-element.4) | data formatting | bytes 1179648
  168.5 0.0 copy-done
  168.5 0.8 copy.18
Async XLA Ops:
  166.5 2.0 %copy-start = (bf16[48,48,128]{2,1,0:T(8,128)(2,1)S(1)}, bf16[48,48,128]{2,1,0:T(8,128)(2,1)}, u32[]{:S(2)}) copy-start(bf16[48,48,128]{2,1,0:T(8,128)(2,1)} %get-tuple-element.5) | copy-start | bytes 1769476

commit v4 on v3

--- a/solution.py
+++ b/solution.py
@@ -25,6 +25,7 @@
 POS = 2 * TILE
 EXP = POS * HEADS
 SUB = 192
+WAVES = (pl.ds(0, 8), pl.ds(8, 16))
 NORM_EPS = 1e-05
 MASKED = -1000000000.0
 INV_ROOT = DIM ** (-0.5)
@@ -212,14 +213,16 @@
         part = lambda k: bias.at[xl, y2, xh, k]
         comes = lambda k: jnp.logical_and(source, k != z)
 
-    def first(d):
-        return send(own_piece, own_piece, p_send.at[d], p_recv.at[z], z_place(d))
+    def first(w, d):
+        region = own_piece.at[WAVES[w]]
+        return send(region, region, p_send.at[w, d], p_recv.at[w, z], z_place(d))
 
     @pl.when(source)
     def _():
         own_piece[...] = piece
-        for d in range(1, 8):
-            first(d).start()
+        for w in range(len(WAVES)):
+            for d in range(1, 8):
+                first(w, d).start()
 
     for r in range(ROWS):
         x_r = rows[:, r].reshape(N, CH)
@@ -251,69 +254,85 @@
         queries(0, r)
         queries(1, r)
 
-    for k in range(8):
-
-        @pl.when(comes(k))
-        def _():
-            send(part(k), part(k), p_send.at[0], p_recv.at[k], sibling).wait_recv()
+    def first_wait(w):
+        for k in range(8):
+
+            @pl.when(comes(k))
+            def _():
+                region = part(k).at[WAVES[w]]
+                send(region, region, p_send.at[w, 0], p_recv.at[w, k], sibling).wait_recv()
 
     x_args = (x_place(1), x_place(-1), g_send, g_recv)
     y_args = (y_place(1), y_place(-1), g_send, g_recv)
-    if starting:
-        a1 = Ring(
-            4, y, lambda k: bias.at[xh, pl.ds(0, 2), xl, k],
-            lambda k: (bias.at[xh, 0, xl, k], bias.at[xh, 1, xl, k]), *y_args, 0,
-        )
-        b1 = Ring(
-            4, x, lambda k: bias.at[k // 2, pl.ds(2, 2), lax.rem(k, 2), y],
-            lambda k: (bias.at[k // 2, 2, lax.rem(k, 2), y], bias.at[k // 2, 3, lax.rem(k, 2), y]), *x_args, 4,
-        )
-        a2 = Ring(
-            4, x, lambda k: bias.at[k // 2, pl.ds(0, 2), lax.rem(k, 2)],
-            lambda k: (bias.at[k // 2, 0, lax.rem(k, 2)], bias.at[k // 2, 1, lax.rem(k, 2)]), *x_args, 8,
-        )
-        b2 = Ring(
-            4, y, lambda k: bias.at[:, pl.ds(2, 2), :, k],
-            lambda k: (bias.at[:, 2, :, k], bias.at[:, 3, :, k]), *y_args, 12,
-        )
-    else:
-        has = lambda k: lax.rem(k, 2) == c
-        here_only = lambda k: source
-        a1 = Ring(
-            4, y, lambda k: bias.at[xl, k // 2, xh, pl.ds(0, 4)],
-            lambda k: (bias.at[xl, k // 2, xh, pl.ds(0, 2)], bias.at[xl, k // 2, xh, pl.ds(2, 2)]), *y_args, 0, has,
-        )
-        b1 = Ring(
-            4, x, lambda k: bias.at[lax.rem(k, 2), y2, k // 2, pl.ds(4, 4)],
-            lambda k: (
-                bias.at[lax.rem(k, 2), y2, k // 2, pl.ds(4, 2)],
-                bias.at[lax.rem(k, 2), y2, k // 2, pl.ds(6, 2)],
-            ), *x_args, 4, here_only,
-        )
-        a2 = Ring(
-            4, x, lambda k: bias.at[lax.rem(k, 2), :, k // 2, pl.ds(0, 4)],
-            lambda k: (
-                bias.at[lax.rem(k, 2), 0, k // 2, pl.ds(0, 4)],
-                bias.at[lax.rem(k, 2), 1, k // 2, pl.ds(0, 4)],
-            ), *x_args, 8,
-        )
-        b2 = Ring(
-            4, y, lambda k: bias.at[:, k // 2, :, pl.ds(4, 4)],
-            lambda k: (bias.at[0, k // 2, :, pl.ds(4, 4)], bias.at[1, k // 2, :, pl.ds(4, 4)]), *y_args, 12, has,
-        )
-
-    a1.start()
-    b1.start()
+    a1, b1, a2, b2 = [], [], [], []
+    for w, rw in enumerate(WAVES):
+        base = 16 * w
+        if starting:
+            a1.append(Ring(
+                4, y, lambda k, rw=rw: bias.at[xh, pl.ds(0, 2), xl, k, rw],
+                lambda k, rw=rw: (bias.at[xh, 0, xl, k, rw], bias.at[xh, 1, xl, k, rw]), *y_args, base,
+            ))
+            b1.append(Ring(
+                4, x, lambda k, rw=rw: bias.at[k // 2, pl.ds(2, 2), lax.rem(k, 2), y, rw],
+                lambda k, rw=rw: (bias.at[k // 2, 2, lax.rem(k, 2), y, rw], bias.at[k // 2, 3, lax.rem(k, 2), y, rw]), *x_args, base + 4,
+            ))
+            a2.append(Ring(
+                4, x, lambda k, rw=rw: bias.at[k // 2, pl.ds(0, 2), lax.rem(k, 2), slice(None), rw],
+                lambda k, rw=rw: (bias.at[k // 2, 0, lax.rem(k, 2), slice(None), rw], bias.at[k // 2, 1, lax.rem(k, 2), slice(None), rw]), *x_args, base + 8,
+            ))
+            b2.append(Ring(
+                4, y, lambda k, rw=rw: bias.at[:, pl.ds(2, 2), :, k, rw],
+                lambda k, rw=rw: (bias.at[:, 2, :, k, rw], bias.at[:, 3, :, k, rw]), *y_args, base + 12,
+            ))
+        else:
+            has = lambda k: lax.rem(k, 2) == c
+            here_only = lambda k: source
+            a1.append(Ring(
+                4, y, lambda k, rw=rw: bias.at[xl, k // 2, xh, pl.ds(0, 4), rw],
+                lambda k, rw=rw: (bias.at[xl, k // 2, xh, pl.ds(0, 2), rw], bias.at[xl, k // 2, xh, pl.ds(2, 2), rw]), *y_args, base, has,
+            ))
+            b1.append(Ring(
+                4, x, lambda k, rw=rw: bias.at[lax.rem(k, 2), y2, k // 2, pl.ds(4, 4), rw],
+                lambda k, rw=rw: (
+                    bias.at[lax.rem(k, 2), y2, k // 2, pl.ds(4, 2), rw],
+                    bias.at[lax.rem(k, 2), y2, k // 2, pl.ds(6, 2), rw],
+                ), *x_args, base + 4, here_only,
+            ))
+            a2.append(Ring(
+                4, x, lambda k, rw=rw: bias.at[lax.rem(k, 2), :, k // 2, pl.ds(0, 4), rw],
+                lambda k, rw=rw: (
+                    bias.at[lax.rem(k, 2), 0, k // 2, pl.ds(0, 4), rw],
+                    bias.at[lax.rem(k, 2), 1, k // 2, pl.ds(0, 4), rw],
+                ), *x_args, base + 8,
+            ))
+            b2.append(Ring(
+                4, y, lambda k, rw=rw: bias.at[:, k // 2, :, pl.ds(4, 4), rw],
+                lambda k, rw=rw: (bias.at[0, k // 2, :, pl.ds(4, 4), rw], bias.at[1, k // 2, :, pl.ds(4, 4), rw]), *y_args, base + 12, has,
+            ))
+
+    both = range(len(WAVES))
+    def phase_a(w):
+        first_wait(w)
+        a1[w].start()
+        b1[w].start()
+
+    phase_a(0)
     for r in range(ROWS):
         queries(2, r)
-    a1.advance(1)
-    b1.advance(1)
+    a1[0].advance(1)
+    b1[0].advance(1)
+    phase_a(1)
+    a1[0].advance(2)
+    b1[0].advance(2)
+    a2[0].start()
+    b2[0].start()
     for r in range(ROWS):
         queries(3, r)
-    a1.advance(2)
-    b1.advance(2)
-    a2.start()
-    b2.start()
+    for step in (1, 2):
+        a1[1].advance(step)
+        b1[1].advance(step)
+    a2[1].start()
+    b2[1].start()
 
     if starting:
         line_at = TILE * (8 * xh + z)
@@ -339,20 +358,23 @@
 
         @pl.when(t == 1)
         def _():
-            a2.advance(1)
-            if starting:
-                b2.advance(1)
+            for w in both:
+                a2[w].advance(1)
+                if starting:
+                    b2[w].advance(1)
 
         @pl.when(t == 2)
         def _():
             if not starting:
-                b2.advance(2)
+                for w in both:
+                    b2[w].advance(2)
 
         @pl.when(t == 3)
         def _():
-            a2.advance(2)
-            if starting:
-                b2.advance(2)
+            for w in both:
+                a2[w].advance(2)
+                if starting:
+                    b2[w].advance(2)
 
         xc = lax.rem(x + step, 4)
         if starting:
@@ -363,7 +385,8 @@
 
             @pl.when(t == 0)
             def _():
-                b2.advance(1)
+                for w in both:
+                    b2[w].advance(1)
 
             y_c = jnp.where(t < 2, y2, 1 - y2)
             attend((lax.rem(t, 2), y_c, slice(None), pl.ds(4, 4)))
@@ -371,8 +394,8 @@
     for u in range(SUPER):
         for r in range(ROWS):
             wide = gat[(r, *in_super(u))].reshape(EXP, CH).astype(BF)
-            both = dot(collapse_ref[...], wide, NN).astype(BF)
-            new = dot(both, w_out_ref[...], NN).astype(BF)
+            joined = dot(collapse_ref[...], wide, NN).astype(BF)
+            new = dot(joined, w_out_ref[...], NN).astype(BF)
             upd[2 * u, r] = new[:TILE]
             upd[2 * u + 1, r] = new[TILE:]
 
@@ -439,10 +462,11 @@
 
         @pl.when(source)
         def _():
-            for d in range(1, 8):
-                first(d).wait_send()
-
-        for ring in (a1, b1, a2, b2):
+            for w in both:
+                for d in range(1, 8):
+                    first(w, d).wait_send()
+
+        for ring in (*a1, *b1, *a2, *b2):
             ring.finish()
 
     return finish
@@ -548,7 +572,7 @@
     tile = pltpu.VMEM((TILE, TILE, CH), BF)
     rows = pltpu.VMEM((16, ROWS, TILE, CH), BF)
     wide_rows = pltpu.VMEM((ROWS, 64, 24, CH), F32)
-    sems = [dma((16,)) for _ in range(4)] + [dma((8,)) for _ in range(2)] + [dma((16,)) for _ in range(4)]
+    sems = [dma((16,)) for _ in range(4)] + [dma((2, 8)) for _ in range(2)] + [dma((32,)) for _ in range(2)] + [dma((16,)) for _ in range(2)]
     return pl.pallas_call(
         kernel,
         out_shape=[jax.ShapeDtypeStruct((TILE, TILE, CH), BF)] * 2,

time: 170 us -> 163 us (0.959)
  Pallas kernels: 166 us -> 157 us
    pallas_call x1, Pallas kernels: 166 us -> 157 us  [on_device(): pl.pallas_call(kernel, out_shape=[jax.ShapeDtypeStruct((TILE, TILE, CH),...]
where the time goes in v4:
time: 163 us; the launch traced here: 161 us
  Pallas kernels  157 us (96%)
  local copies, waits for them, and re-layouts  2.8 us (2%)
    pallas_call x1, Pallas kernels, on_device(): pl.pallas_call(kernel, out_shape=[jax.ShapeDtypeStruct((TILE, TILE, CH),...  157 us

profile of v4, /device:TPU:1, one launch (start us, length us, event | category | flops | bytes accessed | tf_op | source)
XLA Modules:
  0.0 160.8 jit_solution(7209562589834310247)
XLA Ops:
  0.6 157.3 %triangle_attention.1 = (bf16[48,48,128]{2,1,0:T(8,128)(2,1)}, bf16[48,48,128]{2,1,0:T(8,128)(2,1)}) custom-call(bf16[48,48,128]{2,1,0:T(8,128)(2,1)} %tile_ref.1, s32[768]{0:T(1024)} %mask_ref.1, s32[768]{0:T(1024)} %mask_ref.1, bf16[128,512]{1,0:T(8,128)(2,1)} %ps_ref.1, bf16[4,128]{1,0:T(4,128)(2,1)} %bitcast.2, bf16[128,128]{1,0:T(8,128)(2,1)} %os_ref.1, ...), custom_call_target="tpu_custom_call" | custom-call | tf_op jit(solution)/shard_map/triangle_attention/pallas_call | solution.py:576
  158.0 0.0 copy-start
  158.0 2.0 %copy.17 = bf16[48,48,128]{2,1,0:T(8,128)(2,1)} copy(bf16[48,48,128]{2,1,0:T(8,128)(2,1)} %get-tuple-element.4) | data formatting | bytes 1179648
  160.0 0.0 copy-done
  160.0 0.8 copy.18
Async XLA Ops:
  158.0 2.0 %copy-start = (bf16[48,48,128]{2,1,0:T(8,128)(2,1)S(1)}, bf16[48,48,128]{2,1,0:T(8,128)(2,1)}, u32[]{:S(2)}) copy-start(bf16[48,48,128]{2,1,0:T(8,128)(2,1)} %get-tuple-element.5) | copy-start | bytes 1769476

commit v5 on v4

--- a/solution.py
+++ b/solution.py
@@ -252,8 +252,6 @@
 
     for r in range(ROWS):
         queries(0, r)
-        queries(1, r)
-
     def first_wait(w):
         for k in range(8):
 
@@ -318,7 +316,7 @@
 
     phase_a(0)
     for r in range(ROWS):
-        queries(2, r)
+        queries(1, r)
     a1[0].advance(1)
     b1[0].advance(1)
     phase_a(1)
@@ -326,13 +324,14 @@
     b1[0].advance(2)
     a2[0].start()
     b2[0].start()
-    for r in range(ROWS):
-        queries(3, r)
     for step in (1, 2):
         a1[1].advance(step)
         b1[1].advance(step)
     a2[1].start()
     b2[1].start()
+    for r in range(ROWS):
+        queries(2, r)
+        queries(3, r)
 
     if starting:
         line_at = TILE * (8 * xh + z)
@@ -352,46 +351,7 @@
             gated = g_exp[(r, *at)].reshape(SUB, CH) * (o[:, :CH] / o[:, CH:])
             gat[(r, *at)] = gated.reshape(*q_exp[(r, *at)].shape)
 
-    @pl.loop(0, 4)
-    def _(t):
-        step = jnp.where(t == 3, 2, jnp.where(t == 2, 3, t))
-
-        @pl.when(t == 1)
-        def _():
-            for w in both:
-                a2[w].advance(1)
-                if starting:
-                    b2[w].advance(1)
-
-        @pl.when(t == 2)
-        def _():
-            if not starting:
-                for w in both:
-                    b2[w].advance(2)
-
-        @pl.when(t == 3)
-        def _():
-            for w in both:
-                a2[w].advance(2)
-                if starting:
-                    b2[w].advance(2)
-
-        xc = lax.rem(x + step, 4)
-        if starting:
-            attend((xc // 2, pl.ds(0, 2), lax.rem(xc, 2)))
-            attend((slice(None), pl.ds(2, 2), slice(None), lax.rem(y + step, 4)))
-        else:
-            attend((lax.rem(xc, 2), slice(None), xc // 2, pl.ds(0, 4)))
-
-            @pl.when(t == 0)
-            def _():
-                for w in both:
-                    b2[w].advance(1)
-
-            y_c = jnp.where(t < 2, y2, 1 - y2)
-            attend((lax.rem(t, 2), y_c, slice(None), pl.ds(4, 4)))
-
-    for u in range(SUPER):
+    def collapse(u):
         for r in range(ROWS):
             wide = gat[(r, *in_super(u))].reshape(EXP, CH).astype(BF)
             joined = dot(collapse_ref[...], wide, NN).astype(BF)
@@ -399,66 +359,104 @@
             upd[2 * u, r] = new[:TILE]
             upd[2 * u + 1, r] = new[TILE:]
 
+    back_to = ret.at[pl.ds(take * me, take)]
+
+    def backs(u, at):
+        for blk in (0, 1):
+            q = 2 * u + blk
+            if starting:
+                yield q != me, send(upd.at[q], back_to, r_send.at[2 * at + blk], r_recv.at[me], peer_place(q, c))
+            else:
+                p = 4 * u + 2 * c + blk
+                for core in (0, 1):
+                    yield jnp.logical_or(p != me, c != core), send(
+                        upd.at[q, pl.ds(3 * core, 3)],
+                        back_to,
+                        r_send.at[4 * at + 2 * blk + core],
+                        r_recv.at[me],
+                        peer_place(p, core),
+                    )
+
+    def give(u, at):
+        collapse(u)
+        for other_device, copy in backs(u, at):
+            pl.when(other_device)(copy.start)
+
+    done = (0, 2, 1, 3) if starting else (2 - 2 * xl, 3 - 2 * xl, 2 * xl, 2 * xl + 1)
+
+    @pl.loop(0, 8)
+    def _(h):
+        t = h // 2
+        step = jnp.where(t == 3, 2, jnp.where(t == 2, 3, t))
+        first_kind = lax.rem(h, 2) == 0
+        if not starting:
+            first_kind = jnp.where(h < 6, lax.rem(h, 2), 7 - h) == 0
+        rings = {1: [], 2: [], 5: [], 6: [], 7: []}
+        if starting:
+            rings[2] = [(a2, 1), (b2, 1)]
+            rings[6] = [(a2, 2), (b2, 2)]
+        else:
+            rings[1] = [(b2, 1)]
+            rings[2] = [(a2, 1)]
+            rings[5] = [(b2, 2)]
+            rings[7] = [(a2, 2)]
+        for when, moves in rings.items():
+            if moves:
+
+                @pl.when(h == when)
+                def _():
+                    for ring, move in moves:
+                        for w in both:
+                            ring[w].advance(move)
+
+        xc = lax.rem(x + step, 4)
+
+        @pl.when(first_kind)
+        def _():
+            if starting:
+                attend((xc // 2, pl.ds(0, 2), lax.rem(xc, 2)))
+            else:
+                attend((lax.rem(xc, 2), slice(None), xc // 2, pl.ds(0, 4)))
+
+        @pl.when(jnp.logical_not(first_kind))
+        def _():
+            if starting:
+                attend((slice(None), pl.ds(2, 2), slice(None), lax.rem(y + step, 4)))
+            else:
+                y_c = jnp.where(t < 2, y2, 1 - y2)
+                attend((lax.rem(t, 2), y_c, slice(None), pl.ds(4, 4)))
+
+        @pl.when(h == 6)
+        def _():
+            give(done[0], 0)
+            give(done[1], 1)
+
+    give(done[2], 2)
+    give(done[3], 3)
     if starting:
-        for d in range(1, n_peer):
-            j = peer(d)
-            copy = send(
-                upd.at[j], ret.at[pl.ds(take * me, take)], r_send.at[d], r_recv.at[me], peer_place(j, c)
-            )
-            copy.start()
-            sends.append(copy)
-        ret[pl.ds(take * me, take)] = upd[me]
-        for d in range(1, n_peer):
-            j = peer(d)
-            region = ret.at[pl.ds(take * j, take)]
-            send(region, region, r_send.at[d], r_recv.at[j], sibling).wait_recv()
+        back_to[...] = upd[me]
     else:
         mine = lax.rem(me // 2, 2) == c
-        my_q = 2 * (me // 4) + lax.rem(me, 2)
-        back = []
-        for q in range(8):
-            p = 4 * (q // 2) + 2 * c + q % 2
-            for core in (0, 1):
-                copy = send(
-                    upd.at[q, pl.ds(3 * core, 3)],
-                    ret.at[pl.ds(take * me, take)],
-                    r_send.at[2 * q + core],
-                    r_recv.at[me],
-                    peer_place(p, core),
-                )
-                local = jnp.logical_and(p == me, c == core)
-
-                @pl.when(jnp.logical_not(local))
-                def _():
-                    copy.start()
-
-                back.append((local, copy))
 
         @pl.when(mine)
         def _():
-            ret[pl.ds(take * me, take)] = upd[my_q, pl.ds(3 * c, 3)]
-
-        for d in range(n_peer):
-            j = peer(d)
-            region = ret.at[pl.ds(take * j, take)]
-            come = send(region, region, r_send.at[d], r_recv.at[j], sibling)
-            if d == 0:
-
-                @pl.when(jnp.logical_not(mine))
-                def _():
-                    come.wait_recv()
-
-            else:
-                come.wait_recv()
-        for local, copy in back:
-
-            @pl.when(jnp.logical_not(local))
-            def _():
-                copy.wait_send()
+            back_to[...] = upd[2 * (me // 4) + lax.rem(me, 2), pl.ds(3 * c, 3)]
+
+    for d in range(n_peer):
+        j = peer(d)
+        region = ret.at[pl.ds(take * j, take)]
+        come = send(region, region, r_send.at[d], r_recv.at[j], sibling)
+        if d:
+            come.wait_recv()
+        elif not starting:
+            pl.when(jnp.logical_not(mine))(come.wait_recv)
 
     def finish():
         for copy in sends:
             copy.wait_send()
+        for at, u in enumerate(done):
+            for other_device, copy in backs(u, at):
+                pl.when(other_device)(copy.wait_send)
 
         @pl.when(source)
         def _():

time: 163 us -> 162 us (level)
  no operation moved by 1% of the time
where the time goes in v5:
time: 162 us; the launch traced here: 160 us
  Pallas kernels  157 us (97%)
  local copies, waits for them, and re-layouts  2.8 us (2%)
    pallas_call x1, Pallas kernels, on_device(): pl.pallas_call(kernel, out_shape=[jax.ShapeDtypeStruct((TILE, TILE, CH),...  157 us

profile of v5, /device:TPU:1, one launch (start us, length us, event | category | flops | bytes accessed | tf_op | source)
XLA Modules:
  0.0 160.3 jit_solution(9723643004407664748)
XLA Ops:
  0.6 156.9 %triangle_attention.1 = (bf16[48,48,128]{2,1,0:T(8,128)(2,1)}, bf16[48,48,128]{2,1,0:T(8,128)(2,1)}) custom-call(bf16[48,48,128]{2,1,0:T(8,128)(2,1)} %tile_ref.1, s32[768]{0:T(1024)} %mask_ref.1, s32[768]{0:T(1024)} %mask_ref.1, bf16[128,512]{1,0:T(8,128)(2,1)} %ps_ref.1, bf16[4,128]{1,0:T(4,128)(2,1)} %bitcast.2, bf16[128,128]{1,0:T(8,128)(2,1)} %os_ref.1, ...), custom_call_target="tpu_custom_call" | custom-call | tf_op jit(solution)/shard_map/triangle_attention/pallas_call | solution.py:574
  157.5 0.0 copy-start
  157.5 2.0 %copy.17 = bf16[48,48,128]{2,1,0:T(8,128)(2,1)} copy(bf16[48,48,128]{2,1,0:T(8,128)(2,1)} %get-tuple-element.4) | data formatting | bytes 1179648
  159.5 0.0 copy-done
  159.5 0.8 copy.18
Async XLA Ops:
  157.5 2.0 %copy-start = (bf16[48,48,128]{2,1,0:T(8,128)(2,1)S(1)}, bf16[48,48,128]{2,1,0:T(8,128)(2,1)}, u32[]{:S(2)}) copy-start(bf16[48,48,128]{2,1,0:T(8,128)(2,1)} %get-tuple-element.5) | copy-start | bytes 1769476

commit v6 on v5

--- a/solution.py
+++ b/solution.py
@@ -384,52 +384,81 @@
 
     done = (0, 2, 1, 3) if starting else (2 - 2 * xl, 3 - 2 * xl, 2 * xl, 2 * xl + 1)
 
-    @pl.loop(0, 8)
-    def _(h):
-        t = h // 2
-        step = jnp.where(t == 3, 2, jnp.where(t == 2, 3, t))
-        first_kind = lax.rem(h, 2) == 0
-        if not starting:
-            first_kind = jnp.where(h < 6, lax.rem(h, 2), 7 - h) == 0
-        rings = {1: [], 2: [], 5: [], 6: [], 7: []}
-        if starting:
-            rings[2] = [(a2, 1), (b2, 1)]
-            rings[6] = [(a2, 2), (b2, 2)]
-        else:
-            rings[1] = [(b2, 1)]
-            rings[2] = [(a2, 1)]
-            rings[5] = [(b2, 2)]
-            rings[7] = [(a2, 2)]
-        for when, moves in rings.items():
-            if moves:
-
-                @pl.when(h == when)
-                def _():
-                    for ring, move in moves:
-                        for w in both:
-                            ring[w].advance(move)
-
-        xc = lax.rem(x + step, 4)
-
-        @pl.when(first_kind)
-        def _():
+    if starting:
+
+        def last(step):
+            xc = lax.rem(x + step, 4)
+            return (
+                (xc // 2, pl.ds(0, 2), lax.rem(xc, 2)),
+                (slice(None), pl.ds(2, 2), slice(None), lax.rem(y + step, 4)),
+            )
+
+        @pl.loop(0, 3)
+        def _(t):
+            @pl.when(t == 1)
+            def _():
+                for w in both:
+                    a2[w].advance(1)
+                    b2[w].advance(1)
+
+            for spot in last(jnp.where(t == 2, 3, t)):
+                attend(spot)
+
+        for w in both:
+            a2[w].advance(2)
+            b2[w].advance(2)
+        attend(last(2)[0])
+        give(done[0], 0)
+        give(done[1], 1)
+        attend(last(2)[1])
+    else:
+
+        @pl.loop(0, 8)
+        def _(h):
+            t = h // 2
+            step = jnp.where(t == 3, 2, jnp.where(t == 2, 3, t))
+            first_kind = lax.rem(h, 2) == 0
+            if not starting:
+                first_kind = jnp.where(h < 6, lax.rem(h, 2), 7 - h) == 0
+            rings = {1: [], 2: [], 5: [], 6: [], 7: []}
             if starting:
-                attend((xc // 2, pl.ds(0, 2), lax.rem(xc, 2)))
+                rings[2] = [(a2, 1), (b2, 1)]
+                rings[6] = [(a2, 2), (b2, 2)]
             else:
-                attend((lax.rem(xc, 2), slice(None), xc // 2, pl.ds(0, 4)))
-
-        @pl.when(jnp.logical_not(first_kind))
-        def _():
-            if starting:
-                attend((slice(None), pl.ds(2, 2), slice(None), lax.rem(y + step, 4)))
-            else:
-                y_c = jnp.where(t < 2, y2, 1 - y2)
-                attend((lax.rem(t, 2), y_c, slice(None), pl.ds(4, 4)))
-
-        @pl.when(h == 6)
-        def _():
-            give(done[0], 0)
-            give(done[1], 1)
+                rings[1] = [(b2, 1)]
+                rings[2] = [(a2, 1)]
+                rings[5] = [(b2, 2)]
+                rings[7] = [(a2, 2)]
+            for when, moves in rings.items():
+                if moves:
+
+                    @pl.when(h == when)
+                    def _():
+                        for ring, move in moves:
+                            for w in both:
+                                ring[w].advance(move)
+
+            xc = lax.rem(x + step, 4)
+
+            @pl.when(first_kind)
+            def _():
+                if starting:
+                    attend((xc // 2, pl.ds(0, 2), lax.rem(xc, 2)))
+                else:
+                    attend((lax.rem(xc, 2), slice(None), xc // 2, pl.ds(0, 4)))
+
+            @pl.when(jnp.logical_not(first_kind))
+            def _():
+                if starting:
+                    attend((slice(None), pl.ds(2, 2), slice(None), lax.rem(y + step, 4)))
+                else:
+                    y_c = jnp.where(t < 2, y2, 1 - y2)
+                    attend((lax.rem(t, 2), y_c, slice(None), pl.ds(4, 4)))
+
+            @pl.when(h == 6)
+            def _():
+                give(done[0], 0)
+                give(done[1], 1)
 
     give(done[2], 2)
     give(done[3], 3)

time: 162 us -> 159 us (0.981); the launches traced: 160 us -> 159 us
  no operation moved by 1% of the time
where the time goes in v6:
time: 159 us
  Pallas kernels  156 us (98%)
  local copies, waits for them, and re-layouts  2.8 us (2%)
    pallas_call x1, Pallas kernels, on_device(): pl.pallas_call(kernel, out_shape=[jax.ShapeDtypeStruct((TILE, TILE, CH),...  156 us

profile of v6, /device:TPU:1, one launch (start us, length us, event | category | flops | bytes accessed | tf_op | source)
XLA Modules:
  0.0 159.2 jit_solution(18420226335346912902)
XLA Ops:
  0.6 155.7 %triangle_attention.1 = (bf16[48,48,128]{2,1,0:T(8,128)(2,1)}, bf16[48,48,128]{2,1,0:T(8,128)(2,1)}) custom-call(bf16[48,48,128]{2,1,0:T(8,128)(2,1)} %tile_ref.1, s32[768]{0:T(1024)} %mask_ref.1, s32[768]{0:T(1024)} %mask_ref.1, bf16[128,512]{1,0:T(8,128)(2,1)} %ps_ref.1, bf16[4,128]{1,0:T(4,128)(2,1)} %bitcast.2, bf16[128,128]{1,0:T(8,128)(2,1)} %os_ref.1, ...), custom_call_target="tpu_custom_call" | custom-call | tf_op jit(solution)/shard_map/triangle_attention/pallas_call | solution.py:603
  156.4 0.0 copy-start
  156.4 2.0 %copy.17 = bf16[48,48,128]{2,1,0:T(8,128)(2,1)} copy(bf16[48,48,128]{2,1,0:T(8,128)(2,1)} %get-tuple-element.4) | data formatting | bytes 1179648
  158.3 0.0 copy-done
  158.3 0.8 copy.18
Async XLA Ops:
  156.4 2.0 %copy-start = (bf16[48,48,128]{2,1,0:T(8,128)(2,1)S(1)}, bf16[48,48,128]{2,1,0:T(8,128)(2,1)}, u32[]{:S(2)}) copy-start(bf16[48,48,128]{2,1,0:T(8,128)(2,1)} %get-tuple-element.5) | copy-start | bytes 1769476
